TPU v7x, 128 devices: a whole 4x4x4 slice. The times are simulated.
128 devices in a mesh: dp: 8 (over x, core), expert: 16 (over y, z).
Axes of the slice: x: 4, y: 4, z: 4, core: 2. Of those that a mesh axis runs over, the one named last changes fastest.
Arguments:
- out_grad: bfloat16 [32768, 2048], P(('dp', 'expert')), may hold values from -6 to 6
- expert_ids: int32 [32768, 2], P(('dp', 'expert')), may hold values from 0 to 15, all different within a row; in each aligned block of 256 rows (0 to 255, 256 to 511, ...) at most 64 rows name the same one
- gates: float32 [32768, 2], P(('dp', 'expert')), may hold values from 0.1 to 0.9
- hidden_slots: bfloat16 [8, 16, 16, 64, 3200], P('dp', 'expert'), may hold values from -6 to 6
- weights: bfloat16 [16, 3200, 2048], P('expert', 'dp'), may hold values from -0.109375 to 0.109375
- mom_codes: bfloat16 [16, 3200, 2048], P('expert', 'dp'), may hold values from -1 to 1
- mom_scales: float32 [16, 3200], P('expert', 'dp'), may hold values from 0.02 to 0.5
Outputs:
- hidden_grad: bfloat16 [32768, 2, 3200], P(('dp', 'expert'))
- update_dir: bfloat16 [16, 3200, 2048], P('expert', 'dp')
- new_codes: bfloat16 [16, 3200, 2048], P('expert', 'dp')
- new_scales: float32 [16, 3200], P('expert', 'dp')
Inputs may be any that keep to these rules, and one draw needn't show every extreme that they name: `expert_ids`: in each aligned block of 256 tokens (the tokens of one device) no expert is named by more than 64 tokens; a token names two different experts.
All inputs are finite; a program needn't handle non-finite values. Where the computation divides by a largest or mean magnitude, that divisor is 1e-20 or more.
Results may differ from a plain program's by a relative error of at most 0.012.
Values may be sent and summed in bfloat16 or wider, within the bound.
A program may use at most 128 MiB of HBM per device.

v0:
```python
import math

import jax
import jax.numpy as jnp
from jax import lax
from jax.sharding import PartitionSpec as P

beta_one = 0.9
beta_two = 0.99
epsilon = 1e-06


def local(out_grad, expert_ids, gates, hidden_slots, weights, mom_codes, mom_scales):
    experts = lax.axis_size("expert")
    groups = lax.axis_size("dp")
    tok_local = out_grad.shape[0]
    row_count = tok_local * 2
    width = out_grad.shape[1]
    capacity = hidden_slots.shape[3]
    hidden = hidden_slots.shape[4]
    tokens_all = tok_local * groups * experts
    scaled_rows = (gates[:, :, None] * out_grad[:, None, :].astype(jnp.float32)).astype(
        jnp.bfloat16
    )
    scaled_rows = scaled_rows.reshape(row_count, width)
    route_ids = expert_ids.reshape(row_count)
    onehot = (route_ids[:, None] == jnp.arange(experts, dtype=jnp.int32)[None, :]).astype(jnp.int32)
    slot_pos = jnp.sum((jnp.cumsum(onehot, axis=0) - 1) * onehot, axis=1)
    slot_key = route_ids * capacity + slot_pos
    row_index = jnp.arange(row_count, dtype=jnp.int32)
    matched = slot_key[None, :] == jnp.arange(experts * capacity, dtype=jnp.int32)[:, None]
    source_row = jnp.sum(jnp.where(matched, row_index[None, :], 0), axis=1)
    filled = jnp.any(matched, axis=1)
    picked = jnp.take(scaled_rows, source_row, axis=0)
    send_rows = jnp.where(filled[:, None], picked, jnp.zeros((), jnp.bfloat16)).reshape(
        experts, capacity, width
    )
    hidden_table = hidden_slots.reshape(experts * capacity, hidden)
    received = lax.all_to_all(send_rows, "expert", split_axis=0, concat_axis=0, tiled=True)
    flat_rows = received.reshape(experts * capacity, width)
    slot_hidden = jnp.einsum(
        "rd,fd->rf",
        flat_rows,
        lax.all_gather(weights, "dp", axis=1, tiled=True)[0],
        preferred_element_type=jnp.float32,
    ).astype(jnp.bfloat16)
    returned = lax.all_to_all(
        slot_hidden.reshape(experts, capacity, hidden),
        "expert",
        split_axis=0,
        concat_axis=0,
        tiled=True,
    )
    hidden_grad = jnp.take(returned.reshape(experts * capacity, hidden), slot_key, axis=0).reshape(
        tok_local, 2, hidden
    )
    grad_term = jnp.einsum("rf,rd->fd", hidden_table, flat_rows, preferred_element_type=jnp.float32)
    summed = lax.psum_scatter(
        grad_term.astype(jnp.bfloat16), "dp", scatter_dimension=0, tiled=True
    ).astype(jnp.float32)
    gradient = math.sqrt(experts / (2.0 * tokens_all)) * summed
    momentum = mom_codes[0].astype(jnp.float32) * mom_scales[0][:, None]
    blended = beta_one * momentum + (1.0 - beta_one) * gradient
    root_mean = jnp.sqrt(jnp.mean(blended * blended, axis=-1, keepdims=True) + epsilon)
    direction = jnp.tanh(blended / root_mean).astype(jnp.bfloat16)
    advanced = beta_two * momentum + (1.0 - beta_two) * gradient
    new_scales = jnp.max(jnp.abs(advanced), axis=-1) + epsilon
    new_codes = (advanced / new_scales[:, None]).astype(jnp.bfloat16)
    return (hidden_grad, direction[None], new_codes[None], new_scales[None])


def solution(mesh):
    in_specs = (
        P(("dp", "expert"), None),
        P(("dp", "expert"), None),
        P(("dp", "expert"), None),
        P("dp", "expert", None, None, None),
        P("expert", "dp", None),
        P("expert", "dp", None),
        P("expert", "dp"),
    )
    out_specs = (
        P(("dp", "expert"), None, None),
        P("expert", "dp", None),
        P("expert", "dp", None),
        P("expert", "dp"),
    )
    return jax.shard_map(local, mesh=mesh, in_specs=in_specs, out_specs=out_specs, check_vma=False)
```

profile of v0, /device:TPU:0, one launch (start us, length us, event | category | flops | bytes accessed | tf_op | source)
XLA Modules:
  0.0 305.8 jit_solution(9380951864803713545)
XLA Ops:
  7.2 0.0 all-gather.2.cloned.1.call-start
  7.2 0.7 all-gather.2.cloned.1.call-update
  7.9 0.0 reduce-scatter.4.cloned.1.call-start
  7.9 0.8 copy.39
  8.8 0.1 reshape.153
  8.9 0.1 eq.39
  9.1 5.3 %mul.94 = f32[256,2,2048]{2,1,0:T(2,128)} broadcast(bf16[256,2048]{1,0:T(8,128)(2,1)} %param.7), dimensions={0,2} | broadcast | bytes 5242880 | tf_op jit(solution)/shard_map/mul | solution.py:22
  14.4 0.0 copy-start.6
  14.4 6.0 %mul.95 = f32[512,2048]{1,0:T(8,128)} reshape(f32[256,2,2048]{2,1,0:T(2,128)} %mul.94) | data formatting | bytes 8388608 | tf_op jit(solution)/shard_map/mul | solution.py:22
  20.4 0.0 copy-done.6
  20.4 0.1 copy.44
  20.5 0.1 mul.92
  20.7 1.2 reduce-window.6
  21.9 0.2 slice_reduce_fusion
  22.1 0.1 fusion.14
  22.2 0.3 select_reduce_fusion
  22.5 0.1 reduce_sum.38
  22.6 0.3 fusion.10
  22.9 0.1 broadcast_in_dim.63
  23.0 3.1 %multiply_convert_fusion = bf16[512,2048]{1,0:T(8,128)(2,1)S(1)} fusion(f32[512,2048]{1,0:T(8,128)} %mul.95, f32[512]{0:T(512)S(1)} %mul.92), kind=kLoop, calls=%fused_computation.20 | loop fusion | flops 2097152 | bytes 6293504 | tf_op jit(solution)/shard_map/convert_element_type | solution.py:22
  26.1 6.0 %gather_fusion = bf16[1024,2048]{1,0:T(8,128)(2,1)} fusion(bf16[512,2048]{1,0:T(8,128)(2,1)S(1)} %multiply_convert_fusion, s32[1024]{0:T(1024)S(1)} %broadcast_clamp_fusion), kind=kCustom, calls=%fused_computation | custom fusion | bytes 8392704 | tf_op jit(solution)/shard_map/jit(_take)/gather | solution.py:34
  32.2 2.7 select_select_fusion
  34.9 58.8 %all_to_all.10 = bf16[16,64,2048]{2,1,0:T(8,128)(2,1)S(1)} all-to-all(bf16[16,64,2048]{2,1,0:T(8,128)(2,1)S(1)} %select_select_fusion), channel_id=1, replica_groups=mesh['dp'=8,'expert'=16] {'expert'}, dimensions={0} | all-to-all | bytes 8388608 | tf_op jit(solution)/shard_map/all_to_all | solution.py:39
  93.7 0.0 copy-start.2
  93.7 2.0 copy-done.2
  95.7 19.8 %fusion.2 = bf16[3200,2048]{0,1:T(8,128)(2,1)} fusion(bf16[1024,2048]{1,0:T(8,128)(2,1)S(1)} %bitcast.53, bf16[1024,3200]{1,0:T(8,128)(2,1)} %bitcast.62), kind=kOutput, calls=%fused_computation.5 | convolution fusion | flops 13428326400 | bytes 23855104 | tf_op jit(solution)/shard_map/rf,rd->fd/dot_general | solution.py:57
  115.4 18.3 %copy.49 = bf16[3200,2048]{1,0:T(8,128)(2,1)} copy(bf16[3200,2048]{0,1:T(8,128)(2,1)} %fusion.2) | data formatting | bytes 26214400
  133.7 0.0 reduce-scatter.4.cloned.1.call-update
  133.8 0.0 all-gather.2.cloned.1.call-done
  133.8 21.2 %fusion.3 = bf16[1024,3200]{1,0:T(8,128)(2,1)} fusion(bf16[1024,2048]{1,0:T(8,128)(2,1)} %bitcast.54, bf16[1,3200,2048]{2,1,0:T(8,128)(2,1)} %all-gather.2.cloned.1.call-done), kind=kOutput, calls=%fused_computation.6 | convolution fusion | flops 13425049600 | bytes 23855104 | tf_op jit(solution)/shard_map/rd,fd->rf/dot_general | solution.py:41
  155.0 0.0 copy-start.3
  155.0 5.0 %all-to-all-start.1 = ((bf16[16,64,3200]{2,1,0:T(8,128)(2,1)}), bf16[16,64,3200]{2,1,0:T(8,128)(2,1)}, u32[]{:S(2)}, u32[]{:S(2)}) async-start(bf16[16,64,3200]{2,1,0:T(8,128)(2,1)} %bitcast.52), calls=%async_computation.1 | async-start | bytes 13107200 | tf_op jit(solution)/shard_map/all_to_all | solution.py:47
  160.0 0.1 reduce_sum.36
  160.1 0.0 copy-done.3
  160.1 0.1 copy.45
  160.3 0.1 mul.97
  160.4 0.1 copy.42
  160.5 0.2 copy.43
  160.7 2.8 copy.46
  163.6 93.6 %all-to-all-done.1 = bf16[16,64,3200]{2,1,0:T(8,128)(2,1)} async-done(((bf16[16,64,3200]{2,1,0:T(8,128)(2,1)}), bf16[16,64,3200]{2,1,0:T(8,128)(2,1)}, u32[]{:S(2)}, u32[]{:S(2)}) %all-to-all-start.1) | async-done | bytes 6553632 | tf_op jit(solution)/shard_map/all_to_all | solution.py:47
  257.2 10.9 %gather_fusion.1 = bf16[512,3200]{1,0:T(8,128)(2,1)} fusion(bf16[1024,3200]{1,0:T(8,128)(2,1)} %bitcast.7, s32[1024]{0:T(1024)S(1)} %pad_clamp_fusion), kind=kCustom, calls=%fused_computation.1 | custom fusion | bytes 6555648 | tf_op jit(solution)/shard_map/jit(_take)/gather | solution.py:54
  268.1 7.4 %gather.15 = bf16[256,2,3200]{2,1,0:T(2,128)(2,1)} reshape(bf16[512,3200]{1,0:T(8,128)(2,1)} %gather_fusion.1) | data formatting | bytes 6553600 | tf_op jit(solution)/shard_map/jit(_take)/gather | solution.py:54
  275.5 0.0 copy-start.4
  275.5 6.8 %broadcast_select_fusion = bf16[256,2,3200]{2,1,0:T(2,128)(2,1)} fusion(bf16[256,2,3200]{2,1,0:T(2,128)(2,1)} %gather.15, pred[256,2]{1,0:T(8,128)(4,1)S(1)} %copy.43), kind=kLoop, calls=%fused_computation.7 | loop fusion | flops 1638400 | bytes 6554112 | tf_op jit(solution)/shard_map/jit(_take)/select_n | solution.py:54
  282.4 0.0 reduce-scatter.4.cloned.1.call-done
  282.4 3.8 %copy.50 = bf16[400,2048]{0,1:T(8,128)(2,1)} copy(bf16[400,2048]{1,0:T(8,128)(2,1)} %reduce-scatter.4.cloned.1.call-done) | data formatting | bytes 3276800
  286.1 0.0 copy-start
  286.1 0.0 copy-done.4
  286.1 3.4 %abs_reduce_fusion = (f32[400]{0:T(512)S(1)}, f32[400]{0:T(512)S(1)}) fusion(bf16[400,2048]{0,1:T(8,128)(2,1)} %copy.50, bf16[1,400,2048]{1,2,0:T(8,128)(2,1)S(1)} %copy.46, f32[400]{0:T(512)S(1)} %bitcast.58), kind=kLoop, calls=%fused_computation.16 | loop fusion | flops 10648800 | bytes 3281600 | tf_op jit(solution)/shard_map/reduce_max | solution.py:67
  289.6 0.0 copy-start.5
  289.6 0.0 copy-done
  289.6 3.2 %fusion.12 = (bf16[1,400,2048]{1,2,0:T(8,128)(2,1)}, bf16[1,400,2048]{1,2,0:T(8,128)(2,1)}) fusion(f32[400]{0:T(512)S(1)} %get-tuple-element.29, bf16[400,2048]{0,1:T(8,128)(2,1)S(1)} %copy-done, f32[400]{0:T(512)S(1)} %bitcast.59, bf16[1,400,2048]{1,2,0:T(8,128)(2,1)S(1)} %copy.46, f32[400]{0:T(512)S(1)} %get-tuple-element.28), kind=kLoop, calls=%fused_computation.25 | loop fusion | flops 10649600 | bytes 6558400 | tf_op jit(solution)/shard_map/broadcast_in_dim | solution.py:69
  292.8 0.0 copy-done.5
  292.8 0.0 copy-start.1
  292.8 4.0 %copy.47 = bf16[1,400,2048]{2,1,0:T(8,128)(2,1)} copy(bf16[1,400,2048]{1,2,0:T(8,128)(2,1)} %get-tuple-element.27) | data formatting | bytes 3276800
  296.8 0.0 copy-done.1
  296.8 2.2 copy.48
  (12 shorter events, 0.1 us)
Async XLA Ops:
  7.2 126.6 %all-gather.2.cloned.1.call-start = ((), (), s32[]{:S(2)}) async-start(), calls=%async_computation.3 | async-start | bytes 14745600 | tf_op jit(solution)/shard_map/all_gather | solution.py:44
  7.9 274.5 %reduce-scatter.4.cloned.1.call-start = ((), (), s32[]{:S(2)}) async-start(), calls=%async_computation.4 | async-start | bytes 14745600
  14.4 6.0 %copy-start.6 = (f32[256,2]{0,1:T(2,128)S(1)}, f32[256,2]{0,1:T(2,128)}, u32[]{:S(2)}) copy-start(f32[256,2]{0,1:T(2,128)} %param.9) | copy-start | bytes 6148
  93.7 2.0 copy-start.2
  155.0 5.1 %copy-start.3 = (s32[256,2]{0,1:T(2,128)S(1)}, s32[256,2]{0,1:T(2,128)}, u32[]{:S(2)}) copy-start(s32[256,2]{0,1:T(2,128)} %param.8) | copy-start | bytes 6148
  155.0 102.2 %all-to-all-start.1 = ((bf16[16,64,3200]{2,1,0:T(8,128)(2,1)}), bf16[16,64,3200]{2,1,0:T(8,128)(2,1)}, u32[]{:S(2)}, u32[]{:S(2)}) async-start(bf16[16,64,3200]{2,1,0:T(8,128)(2,1)} %bitcast.52), calls=%async_computation.1 | async-start | bytes 13107200 | tf_op jit(solution)/shard_map/all_to_all | solution.py:47
  275.5 10.6 %copy-start.4 = (f32[1,400]{1,0:T(1,128)S(1)}, f32[1,400]{1,0:T(1,128)}, u32[]{:S(2)}) copy-start(f32[1,400]{1,0:T(1,128)} %param.13) | copy-start | bytes 4804
  286.1 3.5 %copy-start = (bf16[400,2048]{0,1:T(8,128)(2,1)S(1)}, bf16[400,2048]{0,1:T(8,128)(2,1)}, u32[]{:S(2)}) copy-start(bf16[400,2048]{0,1:T(8,128)(2,1)} %copy.50) | copy-start | bytes 4915204
  289.6 3.2 %copy-start.5 = (f32[400]{0:T(512)}, f32[400]{0:T(512)S(1)}, u32[]{:S(2)}) copy-start(f32[400]{0:T(512)S(1)} %get-tuple-element.29) | copy-start | bytes 4804
  292.8 4.0 %copy-start.1 = (bf16[1,400,2048]{1,2,0:T(8,128)(2,1)S(1)}, bf16[1,400,2048]{1,2,0:T(8,128)(2,1)}, u32[]{:S(2)}) copy-start(bf16[1,400,2048]{1,2,0:T(8,128)(2,1)} %get-tuple-element.26) | copy-start | bytes 4915204
Sparse Core Ops, SparseCore 0:
  9.7 71.9 all-gather.1
  133.9 73.4 reduce-scatter.3
where the time goes:
time: 310 us; the launch traced here: 306 us
  waiting for transfers between devices  94.4 us (30%)
  local copies, waits for them, and re-layouts  71.2 us (23%)
  blocking collectives  58.8 us (19%)
  matrix products  40.9 us (13%)
  other arithmetic  21.3 us (7%)
  between operations  14.2 us (5%)
  starting transfers between devices  5.06 us (2%)
    all_to_all x1, waiting for transfers between devices, local(): lax.all_to_all(slot_hidden.reshape(experts, capacity, hidden), 'expert',...  93.6 us
    all_to_all x1, blocking collectives, local(): lax.all_to_all(send_rows, 'expert', split_axis=0, concat_axis=0, tiled=True)  58.8 us
    unnamed x21, local copies, waits for them, and re-layouts  34 us
    dot_general x1, matrix products, local(): jnp.einsum('rd,fd->rf', flat_rows, lax.all_gather(weights, 'dp', axis=1,...  21.2 us
    dot_general x1, matrix products, local(): jnp.einsum('rf,rd->fd', hidden_table, flat_rows, preferred_element_type=j...  19.8 us
    gather x2, local copies, waits for them, and re-layouts, local(): jnp.take(returned.reshape(experts * capacity, hidden), slot_key, axis=0)  18.3 us
    mul x3, local copies, waits for them, and re-layouts, local(): gates[:, :, None] * out_grad[:, None, :].astype(jnp.float32)  11.5 us
    select_n x2, other arithmetic, local(): jnp.take(returned.reshape(experts * capacity, hidden), slot_key, axis=0)  6.85 us
  transfers between devices with their start and end apart: 3, of which 1 were waited for; matrix products, arithmetic and copies ran while one was open for 38% of the time, Pallas kernels for 0%

commit v1 on v0

v1 whole, which is shorter than its diff:
```python
import functools
import math

import jax
import jax.numpy as jnp
from jax import lax
from jax.experimental import pallas as pl
from jax.experimental.pallas import tpu as pltpu
from jax.sharding import PartitionSpec as P

MESH = pl.DeviceIdType.MESH
bf16 = jnp.bfloat16
f32 = jnp.float32

beta_one = 0.9
beta_two = 0.99
epsilon = 1e-06

D = 2048
FF = 3200
TOK = 256
CAP = 64
HALF = 32
SHARD = 400
CUT = 208
NCH = 5
C = FF // NCH


def slot_keys(ids):
    tok = ids.shape[1]
    expert = lax.broadcasted_iota(jnp.int32, (16, tok), 0)
    c0 = expert == ids[0:1, :]
    c1 = expert == ids[1:2, :]
    cnt = jnp.where(c0 | c1, 1.0, 0.0).astype(bf16)
    before = jnp.where(
        lax.broadcasted_iota(jnp.int32, (tok, tok), 0) < lax.broadcasted_iota(jnp.int32, (tok, tok), 1), 1.0, 0.0
    ).astype(bf16)
    earlier = jnp.dot(cnt, before, preferred_element_type=f32)
    pos0 = jnp.sum(jnp.where(c0, earlier, 0.0), axis=0, keepdims=True).astype(jnp.int32)
    pos1 = jnp.sum(jnp.where(c1, earlier, 0.0), axis=0, keepdims=True).astype(jnp.int32)
    return ids[0:1, :] * CAP + pos0, ids[1:2, :] * CAP + pos1


def rows_of(start, count):
    return pl.ds(pl.multiple_of(start, 16), count)


def main_kernel(
    og, ids, gates, w, hid,
    ret, pieces, m1a, m1b, m2a, m2b,
    sb, rr, ww, ht, hbuf, pb, oo, sr, tt,
    ag_s, ag_r, loc, p1_s, p1_r, p2_s, p2_r, r1_s, r1_r, r2_s, r2_r, rl, sib_s, sib_r, x_s, x_r, hsem,
):
    dp = lax.axis_index("dp")
    ex = lax.axis_index("expert")
    x, c = dp // 2, dp % 2
    y, z = ex // 4, ex % 4

    def dev_x(d):
        return (((x + d) % 4) * 2 + c, ex)

    def dev_y(d):
        return (dp, ((y + d) % 4) * 4 + z)

    def dev_z(d):
        return (dp, y * 4 + (z + d) % 4)

    sibling = (x * 2 + 1 - c, ex)

    barrier = pltpu.get_barrier_semaphore()
    peers = [dev_y(1), dev_y(2), dev_y(3), dev_z(1), dev_z(2), dev_z(3), dev_x(1), dev_x(3), sibling]
    for peer in peers:
        pl.semaphore_signal(barrier, inc=1, device_id=peer, device_id_type=MESH)
    pl.semaphore_wait(barrier, len(peers))

    def remote(src, dst, s, r, device):
        return pltpu.make_async_remote_copy(
            src_ref=src, dst_ref=dst, send_sem=s, recv_sem=r, device_id=device, device_id_type=MESH
        )

    def shard_rows(xx, cc, lo, n):
        return rows_of(((xx % 4) * 2 + cc) * SHARD + lo, n)

    H0 = (0, CUT)
    H1 = (CUT, SHARD - CUT)

    def ag_copy(i, xx, cut, device, own):
        lo, n = cut
        there = ww.at[shard_rows(xx, c, lo, n)]
        src = w.at[pl.ds(lo, n)] if own else there
        return remote(src, there, ag_s.at[i], ag_r.at[i], device)

    ag = [
        ag_copy(0, x, H0, dev_x(1), True),
        ag_copy(1, x, H1, dev_x(1), True),
        ag_copy(2, x, H1, dev_x(3), True),
        ag_copy(3, x, H0, dev_x(3), True),
        ag_copy(4, x + 3, H0, dev_x(1), False),
        ag_copy(5, x + 1, H1, dev_x(3), False),
        ag_copy(6, x, (0, SHARD), sibling, True),
        ag_copy(7, x + 3, H0, sibling, False),
        ag_copy(8, x + 3, H1, sibling, False),
        ag_copy(9, x + 1, H1, sibling, False),
        ag_copy(10, x + 1, H0, sibling, False),
        ag_copy(11, x + 2, H0, sibling, False),
        ag_copy(12, x + 2, H1, sibling, False),
    ]
    w_own = pltpu.make_async_copy(w, ww.at[shard_rows(x, c, 0, SHARD)], loc.at[0])
    for i in (0, 2, 1, 3, 6):
        ag[i].start()
    w_own.start()

    def h_load(j):
        return pltpu.make_async_copy(hid.at[:, pl.ds(pl.multiple_of(j * C, 128), C)], hbuf.at[j % 2], hsem.at[j % 2])

    h_load(0).start()

    key0, key1 = slot_keys(ids[...])
    g0, g1 = gates[0:1, :], gates[1:2, :]

    def build(yy):
        slot = lax.broadcasted_iota(jnp.int32, (4 * CAP, TOK), 0) + yy * (4 * CAP)
        e0, e1 = slot == key0, slot == key1
        pick = jnp.where(e0 | e1, 1.0, 0.0).astype(bf16)
        gate = jnp.sum(jnp.where(e0, g0, 0.0) + jnp.where(e1, g1, 0.0), axis=1, keepdims=True)

        def cols(n, carry):
            at = pl.ds(pl.multiple_of(n * 512, 512), 512)
            rows = jnp.dot(pick, og[:, at], preferred_element_type=f32)
            sb[yy, :, :, at] = (rows * gate).astype(bf16).reshape(4, CAP, 512)
            return carry

        lax.fori_loop(0, 4, cols, 0)

    A = pl.ds(0, HALF)
    B = pl.ds(HALF, HALF)

    def p1a(d):
        return remote(sb.at[(y + d) % 4, :, A, :], m1a.at[y], p1_s.at[d - 1], p1_r.at[d - 1], dev_y(d))

    def p1b(d):
        return remote(sb.at[:, (z + d) % 4, B, :], m1b.at[z], p1_s.at[2 + d], p1_r.at[2 + d], dev_z(d))

    def p2a(j, d):
        sy = (y + 4 - j) % 4
        src = sb.at[y, (z + d) % 4, A, :] if j == 0 else m1a.at[sy, (z + d) % 4]
        i = j * 3 + d - 1
        return remote(src, rr.at[sy, z, A, :], p2_s.at[i], p2_r.at[i], dev_z(d))

    def p2b(j, d):
        sz = (z + 4 - j) % 4
        src = sb.at[(y + d) % 4, z, B, :] if j == 0 else m1b.at[sz, (y + d) % 4]
        i = 12 + j * 3 + d - 1
        return remote(src, rr.at[y, sz, B, :], p2_s.at[i], p2_r.at[i], dev_y(d))

    def p2a_own(j):
        sy = (y + 4 - j) % 4
        return pltpu.make_async_copy(m1a.at[sy, z], rr.at[sy, z, A, :], loc.at[1 + j])

    def p2b_own(j):
        sz = (z + 4 - j) % 4
        return pltpu.make_async_copy(m1b.at[sz, y], rr.at[y, sz, B, :], loc.at[4 + j])

    own_rows = pltpu.make_async_copy(sb.at[y, z], rr.at[y, z], loc.at[1])

    for d in (1, 3, 2):
        build((y + d) % 4)
        p1a(d).start()
    build(y)
    for d in (1, 3, 2):
        p1b(d).start()
    for d in (1, 3, 2):
        p2a(0, d).start()
        p2b(0, d).start()
    own_rows.start()

    def transpose_chunk(j):
        h_load(j).wait()
        if j + 1 < NCH:
            h_load(j + 1).start()

        def part(i, carry):
            at = pl.ds(pl.multiple_of(i * 128, 128), 128)
            ht[pl.ds(pl.multiple_of(j * C + i * 128, 128), 128), :] = hbuf[j % 2, :, at].T
            return carry

        lax.fori_loop(0, C // 128, part, 0)

    transpose_chunk(0)
    transpose_chunk(1)
    transpose_chunk(2)

    ag[0].wait_recv()
    ag[4].start()
    ag[7].start()
    ag[2].wait_recv()
    ag[5].start()
    ag[9].start()
    transpose_chunk(3)
    transpose_chunk(4)

    for j in (1, 3, 2):
        p1a(j).wait_recv()
        for d in (1, 3, 2):
            p2a(j, d).start()
        p2a_own(j).start()
        p1b(j).wait_recv()
        for d in (1, 3, 2):
            p2b(j, d).start()
        p2b_own(j).start()

    ag[1].wait_recv()
    ag[8].start()
    ag[3].wait_recv()
    ag[10].start()
    ag[4].wait_recv()
    ag[11].start()
    ag[5].wait_recv()
    ag[12].start()

    own_rows.wait()
    for j in (0, 1, 3, 2):
        for d in (1, 3, 2):
            p2a(j, d).wait_recv()
            p2b(j, d).wait_recv()
        if j:
            p2a_own(j).wait()
            p2b_own(j).wait()
    w_own.wait()
    for i in range(6, 13):
        ag[i].wait_recv()

    def product_a(j):
        wj = ww[pl.ds(j * C, C), :]

        def part(i, carry):
            rows = rr[i].reshape(4 * CAP, D)
            res = lax.dot_general(rows, wj, (((1,), (1,)), ((), ())), preferred_element_type=f32)
            oo[j, i] = res.astype(bf16).reshape(4, CAP, C)
            return carry

        lax.fori_loop(0, 4, part, 0)

    def product_b(j):
        hj = ht[pl.ds(j * C, C), :]

        def part(n, carry):
            at = pl.ds(pl.multiple_of(n * 256, 256), 256)
            rows = rr[:, :, :, at].reshape(16 * CAP, 256)
            pb[pl.ds(j * C, C), at] = jnp.dot(hj, rows, preferred_element_type=f32).astype(bf16)
            return carry

        lax.fori_loop(0, D // 256, part, 0)

    def r1a(j, d):
        return remote(oo.at[j, (y + d) % 4, :, A, :], m2a.at[j, y], r1_s.at[j, d - 1], r1_r.at[j, d - 1], dev_y(d))

    def r1b(j, d):
        return remote(oo.at[j, :, (z + d) % 4, B, :], m2b.at[j, z], r1_s.at[j, 2 + d], r1_r.at[j, 2 + d], dev_z(d))

    def r1a_own(j):
        return pltpu.make_async_copy(oo.at[j, y, :, A, :], m2a.at[j, y], rl.at[j, 0])

    def r1b_own(j):
        return pltpu.make_async_copy(oo.at[j, :, z, B, :], m2b.at[j, z], rl.at[j, 1])

    def r2a(j, d):
        return remote(
            m2a.at[j, :, (z + d) % 4], ret.at[j, :, z, A, :], r2_s.at[j, d - 1], r2_r.at[j, d - 1], dev_z(d)
        )

    def r2b(j, d):
        return remote(
            m2b.at[j, :, (y + d) % 4], ret.at[j, y, :, B, :], r2_s.at[j, 2 + d], r2_r.at[j, 2 + d], dev_y(d)
        )

    def r2a_own(j):
        return pltpu.make_async_copy(m2a.at[j, :, z], ret.at[j, :, z, A, :], rl.at[j, 2])

    def r2b_own(j):
        return pltpu.make_async_copy(m2b.at[j, :, y], ret.at[j, y, :, B, :], rl.at[j, 3])

    def send(j):
        for d in (1, 3, 2):
            r1a(j, d).start()
            r1b(j, d).start()
        r1a_own(j).start()
        r1b_own(j).start()

    def forward(j):
        r1a_own(j).wait()
        for d in (1, 3, 2):
            r1a(j, d).wait_recv()
        for d in (1, 3, 2):
            r2a(j, d).start()
        r2a_own(j).start()
        r1b_own(j).wait()
        for d in (1, 3, 2):
            r1b(j, d).wait_recv()
        for d in (1, 3, 2):
            r2b(j, d).start()
        r2b_own(j).start()

    hop = (2, 1, 3, 0)

    def to_sibling(k):
        return remote(pb.at[shard_rows(x + hop[k], 1 - c, 0, SHARD)], sr.at[k], sib_s.at[k], sib_r.at[k], sibling)

    def add_sibling(k):
        to_sibling(k).wait_recv()

        def part(i, carry):
            at = shard_rows(x + hop[k], c, i * 80, 80)
            mine = pb[at, :].astype(f32) + sr[k, pl.ds(pl.multiple_of(i * 80, 16), 80), :].astype(f32)
            pb[at, :] = mine.astype(bf16)
            return carry

        lax.fori_loop(0, SHARD // 80, part, 0)

    def far(i):
        lo, n = (H0, H1)[i]
        return remote(
            pb.at[shard_rows(x + 2, c, lo, n)], tt.at[pl.ds(lo, n)], x_s.at[i], x_r.at[i], dev_x((1, 3)[i])
        )

    def add_far(i):
        far(i).wait_recv()
        lo, n = (H0, H1)[i]

        def part(k, carry):
            at = shard_rows(x + (1, 3)[i], c, lo + k * 16, 16)
            mine = pb[at, :].astype(f32) + tt[pl.ds(pl.multiple_of(lo + k * 16, 16), 16), :].astype(f32)
            pb[at, :] = mine.astype(bf16)
            return carry

        lax.fori_loop(0, n // 16, part, 0)

    def near(i, h):
        lo, n = (H0, H1)[h]
        k = 2 + 2 * i + h
        return remote(
            pb.at[shard_rows(x + (1, 3)[i], c, lo, n)],
            pieces.at[1 + i, pl.ds(lo, n)],
            x_s.at[k],
            x_r.at[k],
            dev_x((1, 3)[i]),
        )

    own_piece = pltpu.make_async_copy(pb.at[shard_rows(x, c, 0, SHARD)], pieces.at[0], loc.at[8])

    product_a(0)
    send(0)
    product_a(1)
    send(1)
    product_b(0)
    product_b(1)
    forward(0)
    product_b(2)
    product_b(3)
    product_b(4)
    for k in range(4):
        to_sibling(k).start()
    product_a(2)
    send(2)
    forward(1)
    add_sibling(0)
    far(0).start()
    far(1).start()
    add_sibling(1)
    near(0, 1).start()
    add_sibling(2)
    near(1, 0).start()
    product_a(3)
    send(3)
    add_sibling(3)
    own_piece.start()
    product_a(4)
    send(4)
    forward(2)
    add_far(0)
    near(0, 0).start()
    add_far(1)
    near(1, 1).start()
    forward(3)
    forward(4)

    for i in range(13):
        ag[i].wait_send()
    for d in (1, 2, 3):
        p1a(d).wait_send()
        p1b(d).wait_send()
        for j in range(4):
            p2a(j, d).wait_send()
            p2b(j, d).wait_send()
    for k in range(4):
        to_sibling(k).wait_send()
    own_piece.wait()
    for i in range(2):
        far(i).wait_send()
        for h in range(2):
            near(i, h).wait()
    for j in range(NCH):
        r2a_own(j).wait()
        r2b_own(j).wait()
        for d in (1, 2, 3):
            r1a(j, d).wait_send()
            r1b(j, d).wait_send()
            r2a(j, d).wait()
            r2b(j, d).wait()


def main_call(og, ids, gates, w, hid):
    any_spec = pl.BlockSpec(memory_space=pl.ANY)
    vmem = pl.BlockSpec(memory_space=pltpu.VMEM)
    dma = pltpu.SemaphoreType.DMA
    s = jax.ShapeDtypeStruct
    return pl.pallas_call(
        main_kernel,
        out_shape=(
            s((NCH, 4, 4, CAP, C), bf16),
            s((3, SHARD, D), bf16),
            s((4, 4, HALF, D), bf16),
            s((4, 4, HALF, D), bf16),
            s((NCH, 4, 4, HALF, C), bf16),
            s((NCH, 4, 4, HALF, C), bf16),
        ),
        in_specs=[vmem, vmem, vmem, any_spec, any_spec],
        out_specs=[any_spec] * 6,
        scratch_shapes=[
            pltpu.VMEM((4, 4, CAP, D), bf16),
            pltpu.VMEM((4, 4, CAP, D), bf16),
            pltpu.VMEM((FF, D), bf16),
            pltpu.VMEM((FF, 16 * CAP), bf16),
            pltpu.VMEM((2, 16 * CAP, C), bf16),
            pltpu.VMEM((FF, D), bf16),
            pltpu.VMEM((NCH, 4, 4, CAP, C), bf16),
            pltpu.VMEM((4, SHARD, D), bf16),
            pltpu.VMEM((SHARD, D), bf16),
            dma((13,)), dma((13,)), dma((9,)),
            dma((6,)), dma((6,)), dma((24,)), dma((24,)),
            dma((NCH, 6)), dma((NCH, 6)), dma((NCH, 6)), dma((NCH, 6)), dma((NCH, 4)),
            dma((4,)), dma((4,)), dma((6,)), dma((6,)), dma((2,)),
        ],
        compiler_params=pltpu.CompilerParams(
            collective_id=0, has_side_effects=True, vmem_limit_bytes=63 * 2**20
        ),
        cost_estimate=pl.CostEstimate(flops=28 * 10**9, bytes_accessed=50 * 10**6, transcendentals=0),
        name="dispatch_products_return",
    )(og, ids, gates, w, hid)


def pick_kernel(ids, ret, out):
    key0, key1 = slot_keys(ids[...])
    slot = lax.broadcasted_iota(jnp.int32, (16 * CAP, TOK), 0)
    rows = ret[...].reshape(16 * CAP, C)
    for k, key in enumerate((key0, key1)):
        pick = jnp.where(slot == key, 1.0, 0.0).astype(bf16)
        got = lax.dot_general(pick, rows, (((0,), (0,)), ((), ())), preferred_element_type=f32)
        out[:, k, :] = got.astype(bf16)


def pick_call(ids, ret):
    return pl.pallas_call(
        pick_kernel,
        grid=(NCH,),
        out_shape=jax.ShapeDtypeStruct((TOK, 2, FF), bf16),
        in_specs=[
            pl.BlockSpec((2, TOK), lambda j: (0, 0)),
            pl.BlockSpec((None, 4, 4, CAP, C), lambda j: (j, 0, 0, 0, 0)),
        ],
        out_specs=pl.BlockSpec((TOK, 2, C), lambda j: (0, 0, j)),
        compiler_params=pltpu.CompilerParams(vmem_limit_bytes=48 * 2**20),
        name="pick_rows",
    )(ids, ret)


ROWS = 80


def step_kernel(factor, pieces, codes, scales, direction, new_codes, new_scales):
    i = pl.program_id(0)
    gradient = factor * (
        pieces[0].astype(f32) + pieces[1].astype(f32) + pieces[2].astype(f32)
    )
    here = lax.broadcasted_iota(jnp.int32, (ROWS, SHARD), 0) + i * ROWS == lax.broadcasted_iota(
        jnp.int32, (ROWS, SHARD), 1
    )
    scale = jnp.sum(jnp.where(here, scales[...], 0.0), axis=1, keepdims=True)
    momentum = codes[...].astype(f32) * scale
    blended = beta_one * momentum + (1.0 - beta_one) * gradient
    root = jnp.sqrt(jnp.mean(blended * blended, axis=-1, keepdims=True) + epsilon)
    direction[...] = jnp.tanh(blended / root).astype(bf16)
    advanced = beta_two * momentum + (1.0 - beta_two) * gradient
    largest = jnp.max(jnp.abs(advanced), axis=-1, keepdims=True) + epsilon
    new_codes[...] = (advanced / largest).astype(bf16)

    @pl.when(i == 0)
    def _():
        new_scales[...] = jnp.zeros_like(new_scales)

    new_scales[...] += jnp.sum(jnp.where(here, largest, 0.0), axis=0, keepdims=True)


def step_call(factor, pieces, codes, scales):
    block = pl.BlockSpec((ROWS, D), lambda i: (i, 0))
    line = pl.BlockSpec((1, SHARD), lambda i: (0, 0))
    return pl.pallas_call(
        functools.partial(step_kernel, factor),
        grid=(SHARD // ROWS,),
        out_shape=(
            jax.ShapeDtypeStruct((SHARD, D), bf16),
            jax.ShapeDtypeStruct((SHARD, D), bf16),
            jax.ShapeDtypeStruct((1, SHARD), f32),
        ),
        in_specs=[pl.BlockSpec((3, ROWS, D), lambda i: (0, i, 0)), block, line],
        out_specs=(block, block, line),
        compiler_params=pltpu.CompilerParams(vmem_limit_bytes=48 * 2**20),
        name="optimizer_step",
    )(pieces, codes, scales)


def local(out_grad, expert_ids, gates, hidden_slots, weights, mom_codes, mom_scales):
    experts = lax.axis_size("expert")
    groups = lax.axis_size("dp")
    tokens_all = out_grad.shape[0] * groups * experts
    ids = expert_ids.T
    ret, pieces, _, _, _, _ = main_call(
        out_grad, ids, gates.T, weights[0], hidden_slots.reshape(16 * CAP, FF)
    )
    hidden_grad = pick_call(ids, ret)
    factor = math.sqrt(experts / (2.0 * tokens_all))
    direction, new_codes, new_scales = step_call(factor, pieces, mom_codes[0], mom_scales)
    return (hidden_grad, direction[None], new_codes[None], new_scales)


def solution(mesh):
    in_specs = (
        P(("dp", "expert"), None),
        P(("dp", "expert"), None),
        P(("dp", "expert"), None),
        P("dp", "expert", None, None, None),
        P("expert", "dp", None),
        P("expert", "dp", None),
        P("expert", "dp"),
    )
    out_specs = (
        P(("dp", "expert"), None, None),
        P("expert", "dp", None),
        P("expert", "dp", None),
        P("expert", "dp"),
    )
    return jax.shard_map(local, mesh=mesh, in_specs=in_specs, out_specs=out_specs, check_vma=False)
```

time: 310 us -> 174 us (0.56)
  Pallas kernels: 0 us -> 172 us
  waiting for transfers between devices: 94.4 us -> 0 us
  local copies, waits for them, and re-layouts: 71.2 us -> 0.02 us
  blocking collectives: 58.8 us -> 0 us
  matrix products: 40.9 us -> 0 us
  other arithmetic: 21.3 us -> 0 us
  between operations: 14.2 us -> 0.67 us
  starting transfers between devices: 5.06 us -> 0 us
    pallas_call x0 -> x3, Pallas kernels: none -> 172 us  [the longest x1 156 us: main_call(): pl.pallas_call(main_kernel, out_shape=(s((NCH, 4, 4, CAP, C), bf16), s((3...]
    all_to_all x1 -> x0, waiting for transfers between devices: 93.6 us -> none  [local(): lax.all_to_all(slot_hidden.reshape(experts, capacity, hidden), 'expert',...]
    all_to_all x1 -> x0, blocking collectives: 58.8 us -> none  [local(): lax.all_to_all(send_rows, 'expert', split_axis=0, concat_axis=0, tiled=True)]
    dot_general x2 -> x0, matrix products: 40.9 us -> none  [the longest x1 21.2 us: local(): jnp.einsum('rd,fd->rf', flat_rows, lax.all_gather(weights, 'dp', axis=1,...]
    unnamed x21 -> x6, local copies, waits for them, and re-layouts: 34 us -> 0.02 us
    gather x3 -> x0, local copies, waits for them, and re-layouts: 24.4 us -> none  [the longest x2 18.3 us: local(): jnp.take(returned.reshape(experts * capacity, hidden), slot_key, axis=0)]
    mul x5 -> x0, local copies, waits for them, and re-layouts: 11.8 us -> none  [the longest x3 11.5 us: local(): gates[:, :, None] * out_grad[:, None, :].astype(jnp.float32)]
    select_n x4 -> x0, other arithmetic: 9.56 us -> none  [the longest x2 6.85 us: local(): jnp.take(returned.reshape(experts * capacity, hidden), slot_key, axis=0)]
  transfers between devices with their start and end apart: 3 -> 0, of which waited for: 1 -> 0; matrix products, arithmetic and copies ran while one was open for 38% -> 0% of each run, Pallas kernels for 0% -> 0%
where the time goes in v1:
time: 174 us; the launch traced here: 173 us
  Pallas kernels  172 us (99%)
    pallas_call x1, Pallas kernels, main_call(): pl.pallas_call(main_kernel, out_shape=(s((NCH, 4, 4, CAP, C), bf16), s((3...  156 us
    pallas_call x1, Pallas kernels, pick_call(): pl.pallas_call(pick_kernel, grid=(NCH,), out_shape=jax.ShapeDtypeStruct((...  9.42 us
    pallas_call x1, Pallas kernels, step_call(): pl.pallas_call(functools.partial(step_kernel, factor), grid=(SHARD // ROW...  6.72 us

profile of v1, /device:TPU:0, one launch (start us, length us, event | category | flops | bytes accessed | tf_op | source)
XLA Modules:
  0.0 172.7 jit_solution(16728552717525140547)
XLA Ops:
  0.6 0.0 copy-start.2
  0.6 155.8 %dispatch_products_return.1 = (bf16[5,4,4,64,640]{4,3,2,1,0:T(8,128)(2,1)}, bf16[3,400,2048]{2,1,0:T(8,128)(2,1)}, bf16[4,4,32,2048]{3,2,1,0:T(8,128)(2,1)}, bf1...) custom-call(bf16[256,2048]{1,0:T(8,128)(2,1)} %og.1, ...), custom_call_target="tpu_custom_call" | custom-call | flops 28000000000 | bytes 50000000 | tf_op jit(solution)/shard_map/dispatch_products_return/pallas_call | solution.py:418
  156.5 0.0 copy-done.2
  156.5 0.0 copy-start
  156.5 0.0 copy-start.1
  156.5 9.4 %pick_rows.1 = bf16[256,2,3200]{2,1,0:T(2,128)(2,1)} custom-call(s32[2,256]{1,0:T(2,128)S(1)} %bitcast.9, bf16[5,4,4,64,640]{4,3,2,1,0:T(8,128)(2,1)} %get-tuple-element.9.ret), custom_call_target="tpu_custom_call" | custom-call | tf_op jit(solution)/shard_map/pick_rows/pallas_call | solution.py:464
  165.9 0.0 copy-done
  165.9 0.0 copy-done.1
  165.9 6.7 %optimizer_step.1 = (bf16[400,2048]{1,0:T(8,128)(2,1)}, bf16[400,2048]{1,0:T(8,128)(2,1)}, f32[1,400]{1,0:T(1,128)}) custom-call(bf16[3,400,2048]{2,1,0:T(8,128)(2,1)} %get-tuple-element.10.pieces, bf16[400,2048]{1,0:T(8,128)(2,1)S(1)} %bitcast.7, f32[1,400]{1,0:T(1,128)S(1)} %copy-done.1), custom_call_target="tpu_custom_call" | custom-call | tf_op jit(solution)/shard_map/optimizer_step/pallas_call | solution.py:508
Async XLA Ops:
  0.6 155.9 %copy-start.2 = (s32[256,2]{0,1:T(2,128)S(1)}, s32[256,2]{0,1:T(2,128)}, u32[]{:S(2)}) copy-start(s32[256,2]{0,1:T(2,128)} %param.8) | copy-start | bytes 6148
  156.5 9.4 %copy-start = (bf16[1,400,2048]{2,1,0:T(8,128)(2,1)S(1)}, bf16[1,400,2048]{2,1,0:T(8,128)(2,1)}, u32[]{:S(2)}) copy-start(bf16[1,400,2048]{2,1,0:T(8,128)(2,1)} %param.12) | copy-start | bytes 4915204
  156.5 9.4 %copy-start.1 = (f32[1,400]{1,0:T(1,128)S(1)}, f32[1,400]{1,0:T(1,128)}, u32[]{:S(2)}) copy-start(f32[1,400]{1,0:T(1,128)} %scales.1) | copy-start | bytes 4804

commit v2 on v1

v2 whole, which is shorter than its diff:
```python
import functools
import math

import jax
import jax.numpy as jnp
from jax import lax
from jax.experimental import pallas as pl
from jax.experimental.pallas import tpu as pltpu
from jax.sharding import PartitionSpec as P

MESH = pl.DeviceIdType.MESH
bf16 = jnp.bfloat16
f32 = jnp.float32

beta_one = 0.9
beta_two = 0.99
epsilon = 1e-06

D = 2048
FF = 3200
TOK = 256
CAP = 64
HALF = 32
HD = D // 2
ROWS = 80
SHARD = 400
CUT = 208
NCH = 5
C = FF // NCH


def slot_keys(ids):
    tok = ids.shape[1]
    expert = lax.broadcasted_iota(jnp.int32, (16, tok), 0)
    c0 = expert == ids[0:1, :]
    c1 = expert == ids[1:2, :]
    cnt = jnp.where(c0 | c1, 1.0, 0.0).astype(bf16)
    before = jnp.where(
        lax.broadcasted_iota(jnp.int32, (tok, tok), 0) < lax.broadcasted_iota(jnp.int32, (tok, tok), 1), 1.0, 0.0
    ).astype(bf16)
    earlier = jnp.dot(cnt, before, preferred_element_type=f32)
    pos0 = jnp.sum(jnp.where(c0, earlier, 0.0), axis=0, keepdims=True).astype(jnp.int32)
    pos1 = jnp.sum(jnp.where(c1, earlier, 0.0), axis=0, keepdims=True).astype(jnp.int32)
    return ids[0:1, :] * CAP + pos0, ids[1:2, :] * CAP + pos1


def rows_of(start, count):
    return pl.ds(pl.multiple_of(start, 16), count)


def main_kernel(
    factor,
    og, ids, gates, scales, w, hid, codes,
    hidden_grad, direction, new_codes, new_scales,
    ret, pieces, sr, m2a, m2b,
    sa, sb, meta, rr, ww, hv, pb, oo, sums, tt, pk, ost,
    ag_s, ag_r, loc, p1_s, p1_r, mt_s, mt_r, p2_s, p2_r, r1_s, r1_r, r2_s, r2_r, rl, sib_s, sib_r, x_s, x_r, tail_s, own_s,
):
    dp = lax.axis_index("dp")
    ex = lax.axis_index("expert")
    x, c = dp // 2, dp % 2
    y, z = ex // 4, ex % 4

    def dev_x(d):
        return (((x + d) % 4) * 2 + c, ex)

    def dev_y(d):
        return (dp, ((y + d) % 4) * 4 + z)

    def dev_z(d):
        return (dp, y * 4 + (z + d) % 4)

    sibling = (x * 2 + 1 - c, ex)

    barrier = pltpu.get_barrier_semaphore()
    peers = [dev_y(1), dev_y(2), dev_y(3), dev_z(1), dev_z(2), dev_z(3), dev_x(1), dev_x(3), sibling]
    for peer in peers:
        pl.semaphore_signal(barrier, inc=1, device_id=peer, device_id_type=MESH)
    pl.semaphore_wait(barrier, len(peers))

    def remote(src, dst, s, r, device):
        return pltpu.make_async_remote_copy(
            src_ref=src, dst_ref=dst, send_sem=s, recv_sem=r, device_id=device, device_id_type=MESH
        )

    def shard_rows(xx, cc, lo, n):
        return rows_of(((xx % 4) * 2 + cc) * SHARD + lo, n)

    H0 = (0, CUT)
    H1 = (CUT, SHARD - CUT)

    def ag_copy(i, xx, cut, device, own):
        lo, n = cut
        there = ww.at[shard_rows(xx, c, lo, n)]
        src = w.at[pl.ds(lo, n)] if own else there
        return remote(src, there, ag_s.at[i], ag_r.at[i], device)

    ag = [
        ag_copy(0, x, H0, dev_x(1), True),
        ag_copy(1, x, H1, dev_x(1), True),
        ag_copy(2, x, H1, dev_x(3), True),
        ag_copy(3, x, H0, dev_x(3), True),
        ag_copy(4, x + 3, H0, dev_x(1), False),
        ag_copy(5, x + 1, H1, dev_x(3), False),
        ag_copy(6, x, (0, SHARD), sibling, True),
        ag_copy(7, x + 3, H0, sibling, False),
        ag_copy(8, x + 3, H1, sibling, False),
        ag_copy(9, x + 1, H1, sibling, False),
        ag_copy(10, x + 1, H0, sibling, False),
        ag_copy(11, x + 2, H0, sibling, False),
        ag_copy(12, x + 2, H1, sibling, False),
    ]
    w_own = pltpu.make_async_copy(w, ww.at[shard_rows(x, c, 0, SHARD)], loc.at[0])
    for i in (0, 2, 1, 3, 6):
        ag[i].start()
    w_own.start()

    h_load = pltpu.make_async_copy(hid, hv, loc.at[8])
    h_load.start()

    def og_copy(i, own_axis, d, half, axis):
        pos = (y, z)[axis]
        src_pos = (pos + (0, 0, 0, 0, 3, 1)[i]) % 4
        rows = half * (TOK // 2)
        there = pb.at[rows_of(src_pos * TOK + rows, TOK // 2), pl.ds(axis * HD, HD)]
        src = og.at[pl.ds(rows, TOK // 2), pl.ds(axis * HD, HD)] if own_axis else there
        k = axis * 6 + i
        return remote(src, there, p1_s.at[k], p1_r.at[k], (dev_y, dev_z)[axis](d))

    def og_copies(axis):
        return [
            og_copy(0, True, 1, 0, axis),
            og_copy(1, True, 1, 1, axis),
            og_copy(2, True, 3, 1, axis),
            og_copy(3, True, 3, 0, axis),
            og_copy(4, False, 1, 0, axis),
            og_copy(5, False, 3, 1, axis),
        ]

    oy, oz = og_copies(0), og_copies(1)
    for i in (0, 2, 1, 3):
        oy[i].start()
        oz[i].start()

    key0, key1 = slot_keys(ids[...])
    for axis, pos in ((0, y), (1, z)):
        meta[axis * 4 + pos, 0:1, :] = key0.astype(f32)
        meta[axis * 4 + pos, 1:2, :] = key1.astype(f32)
        meta[axis * 4 + pos, 2:4, :] = gates[...]
        meta[axis * 4 + pos, 4:8, :] = jnp.zeros((4, TOK), f32)

    def meta_copy(axis, d):
        at = meta.at[axis * 4 + (y, z)[axis]]
        k = axis * 3 + d - 1
        return remote(at, at, mt_s.at[k], mt_r.at[k], (dev_y, dev_z)[axis](d))

    for d in (1, 3, 2):
        meta_copy(0, d).start()
        meta_copy(1, d).start()

    def build(axis, j):
        pos = ((y, z)[axis] + 4 - j) % 4
        info = meta[axis * 4 + pos]
        i = lax.broadcasted_iota(jnp.int32, (4 * CAP, TOK), 0)
        slot = i + y * (4 * CAP) if axis == 0 else (i // CAP) * (4 * CAP) + z * CAP + i % CAP
        slot = slot.astype(f32)
        e0, e1 = slot == info[0:1], slot == info[1:2]
        pick = jnp.where(e0 | e1, 1.0, 0.0).astype(bf16)
        gate = jnp.sum(jnp.where(e0, info[2:3], 0.0) + jnp.where(e1, info[3:4], 0.0), axis=1, keepdims=True)
        cols = pl.ds(axis * HD, HD)
        rows = og[:, cols] if j == 0 else pb[rows_of(pos * TOK, TOK), cols]
        res = jnp.dot(pick, rows, preferred_element_type=f32)
        (sa, sb)[axis][pos] = (res * gate).astype(bf16).reshape(4, CAP, HD)

    A = pl.ds(0, HALF)
    B = pl.ds(HALF, HALF)
    left, right = pl.ds(0, HD), pl.ds(HD, HD)

    def p2a(j, d):
        sy = (y + 4 - j) % 4
        i = j * 3 + d - 1
        return remote(sa.at[sy, (z + d) % 4], rr.at[sy, z, :, left], p2_s.at[i], p2_r.at[i], dev_z(d))

    def p2b(j, d):
        sz = (z + 4 - j) % 4
        i = 12 + j * 3 + d - 1
        return remote(sb.at[sz, (y + d) % 4], rr.at[y, sz, :, right], p2_s.at[i], p2_r.at[i], dev_y(d))

    def p2a_own(j):
        sy = (y + 4 - j) % 4
        return pltpu.make_async_copy(sa.at[sy, z], rr.at[sy, z, :, left], own_s.at[j])

    def p2b_own(j):
        sz = (z + 4 - j) % 4
        return pltpu.make_async_copy(sb.at[sz, y], rr.at[y, sz, :, right], own_s.at[4 + j])

    def dispatch(j):
        build(0, j)
        for d in (1, 3, 2):
            p2a(j, d).start()
        p2a_own(j).start()
        build(1, j)
        for d in (1, 3, 2):
            p2b(j, d).start()
        p2b_own(j).start()

    dispatch(0)

    oy[0].wait_recv()
    oy[4].start()
    oz[0].wait_recv()
    oz[4].start()
    oy[2].wait_recv()
    oy[5].start()
    oz[2].wait_recv()
    oz[5].start()
    for j, i in ((1, 1), (3, 3)):
        oy[i].wait_recv()
        oz[i].wait_recv()
        meta_copy(0, j).wait_recv()
        meta_copy(1, j).wait_recv()
        dispatch(j)

    slot_id = lax.broadcasted_iota(jnp.int32, (16 * CAP, TOK), 0)
    pk[0:TOK, :] = jnp.where(slot_id == key0, 1.0, 0.0).astype(bf16).T
    pk[TOK:, :] = jnp.where(slot_id == key1, 1.0, 0.0).astype(bf16).T

    for i in (4, 5):
        oy[i].wait_recv()
        oz[i].wait_recv()
    meta_copy(0, 2).wait_recv()
    meta_copy(1, 2).wait_recv()
    dispatch(2)

    ag[0].wait_recv()
    ag[4].start()
    ag[7].start()
    ag[2].wait_recv()
    ag[5].start()
    ag[9].start()
    ag[1].wait_recv()
    ag[8].start()
    ag[3].wait_recv()
    ag[10].start()

    for j in (0, 1, 3, 2):
        for d in (1, 3, 2):
            p2a(j, d).wait_recv()
            p2b(j, d).wait_recv()
        p2a_own(j).wait()
        p2b_own(j).wait()
    for i in range(6):
        oy[i].wait_send()
        oz[i].wait_send()
    w_own.wait()
    for i in range(6, 11):
        ag[i].wait_recv()
    h_load.wait()

    first = ((x + 2) % 4 + 2) % 5

    def chunk(i):
        return (first + i) % NCH

    def product_a(i):
        wj = ww[rows_of(chunk(i) * C, C), :]
        rows = rr[...].reshape(16 * CAP, D)
        res = lax.dot_general(rows, wj, (((1,), (1,)), ((), ())), preferred_element_type=f32)
        oo[i] = res.astype(bf16).reshape(4, 4, CAP, C)

    def product_b(i):
        at = chunk(i) * C

        def part(n, carry):
            cols = pl.ds(pl.multiple_of(n * 1024, 1024), 1024)
            hj = hv[:, pl.ds(pl.multiple_of(at, 128), C)]
            rows = rr[:, :, :, cols].reshape(16 * CAP, 1024)
            res = lax.dot_general(hj, rows, (((0,), (0,)), ((), ())), preferred_element_type=f32)
            pb[rows_of(at, C), cols] = res.astype(bf16)
            return carry

        lax.fori_loop(0, D // 1024, part, 0)

    def r1a(j, d):
        return remote(oo.at[j, (y + d) % 4, :, A, :], m2a.at[j, y], r1_s.at[j, d - 1], r1_r.at[j, d - 1], dev_y(d))

    def r1b(j, d):
        return remote(oo.at[j, :, (z + d) % 4, B, :], m2b.at[j, z], r1_s.at[j, 2 + d], r1_r.at[j, 2 + d], dev_z(d))

    def r1a_own(j):
        return pltpu.make_async_copy(oo.at[j, y, :, A, :], m2a.at[j, y], rl.at[j, 0])

    def r1b_own(j):
        return pltpu.make_async_copy(oo.at[j, :, z, B, :], m2b.at[j, z], rl.at[j, 1])

    def r2a(j, d):
        return remote(
            m2a.at[j, :, (z + d) % 4], ret.at[chunk(j), :, z, A, :], r2_s.at[j, d - 1], r2_r.at[j, d - 1], dev_z(d)
        )

    def r2b(j, d):
        return remote(
            m2b.at[j, :, (y + d) % 4], ret.at[chunk(j), y, :, B, :], r2_s.at[j, 2 + d], r2_r.at[j, 2 + d], dev_y(d)
        )

    def r2a_own(j):
        return pltpu.make_async_copy(m2a.at[j, :, z], ret.at[chunk(j), :, z, A, :], rl.at[j, 2])

    def r2b_own(j):
        return pltpu.make_async_copy(m2b.at[j, :, y], ret.at[chunk(j), y, :, B, :], rl.at[j, 3])

    def send(j):
        for d in (1, 3, 2):
            r1a(j, d).start()
            r1b(j, d).start()
        r1a_own(j).start()
        r1b_own(j).start()

    def forward(j):
        r1a_own(j).wait()
        for d in (1, 3, 2):
            r1a(j, d).wait_recv()
        for d in (1, 3, 2):
            r2a(j, d).start()
        r2a_own(j).start()
        r1b_own(j).wait()
        for d in (1, 3, 2):
            r1b(j, d).wait_recv()
        for d in (1, 3, 2):
            r2b(j, d).start()
        r2b_own(j).start()

    hop = (2, 1, 3, 0)

    def to_sibling(k):
        return remote(pb.at[shard_rows(x + hop[k], 1 - c, 0, SHARD)], sr.at[k], sib_s.at[k], sib_r.at[k], sibling)

    def add_sibling(k):
        to_sibling(k).wait_recv()
        load = pltpu.make_async_copy(sr.at[k], sums, loc.at[7])
        load.start()
        load.wait()

        def part(i, carry):
            at = shard_rows(x + hop[k], c, i * 80, 80)
            mine = pb[at, :].astype(f32) + sums[rows_of(i * 80, 80), :].astype(f32)
            pb[at, :] = mine.astype(bf16)
            return carry

        lax.fori_loop(0, SHARD // 80, part, 0)

    def far(i):
        lo, n = (H0, H1)[i]
        return remote(
            pb.at[shard_rows(x + 2, c, lo, n)], tt.at[pl.ds(lo, n)], x_s.at[i], x_r.at[i], dev_x((1, 3)[i])
        )

    def add_far(i):
        far(i).wait_recv()
        lo, n = (H0, H1)[i]

        def part(k, carry):
            at = shard_rows(x + (1, 3)[i], c, lo + k * 16, 16)
            mine = pb[at, :].astype(f32) + tt[pl.ds(pl.multiple_of(lo + k * 16, 16), 16), :].astype(f32)
            pb[at, :] = mine.astype(bf16)
            return carry

        lax.fori_loop(0, n // 16, part, 0)

    def near(i, h):
        lo, n = (H0, H1)[h]
        k = 2 + 2 * i + h
        return remote(
            pb.at[shard_rows(x + (1, 3)[i], c, lo, n)],
            pieces.at[i, pl.ds(lo, n)],
            x_s.at[k],
            x_r.at[k],
            dev_x((1, 3)[i]),
        )

    def stage(i):
        buf, at = ((sa, 0), (sb, 0), (rr, 0), (rr, 1), (rr, 2))[i]
        return buf.at[:, :, :, pl.ds(at * C, C)]

    def stage_load(i):
        return pltpu.make_async_copy(ret.at[chunk(i)], stage(i), tail_s.at[i])

    def out_copy(i):
        at = pl.ds(pl.multiple_of(chunk(i) * C, 128), C)
        return pltpu.make_async_copy(ost.at[i % 2], hidden_grad.at[:, :, at], tail_s.at[NCH + i])

    def pick(i):
        r2a_own(i).wait()
        r2b_own(i).wait()
        for d in (1, 3, 2):
            r2a(i, d).wait_recv()
            r2b(i, d).wait_recv()
        stage_load(i).start()
        stage_load(i).wait()
        if i >= 2:
            out_copy(i - 2).wait()
        rows = stage(i)[...].reshape(16 * CAP, C)
        got = jnp.dot(pk[...], rows, preferred_element_type=f32).astype(bf16)
        ost[i % 2, :, 0, :] = got[0:TOK]
        ost[i % 2, :, 1, :] = got[TOK:]
        out_copy(i).start()

    def step_load(k):
        src = (codes, pieces.at[0], pieces.at[1])[k]
        return pltpu.make_async_copy(src, ww.at[pl.ds(k * SHARD, SHARD)], tail_s.at[2 * NCH + k])

    def step_out(k):
        dst = (new_codes, direction)[k]
        return pltpu.make_async_copy(ww.at[pl.ds(k * SHARD, SHARD)], dst, tail_s.at[2 * NCH + 3 + k])

    def step():
        for k in range(3):
            step_load(k).wait()
        new_scales[...] = jnp.zeros_like(new_scales)

        def part(i, carry):
            def of(k):
                return ww[rows_of(k * SHARD + i * ROWS, ROWS), :].astype(f32)

            mine = pb[shard_rows(x, c, i * ROWS, ROWS), :].astype(f32)
            gradient = factor * (mine + of(1) + of(2))
            here = lax.broadcasted_iota(jnp.int32, (ROWS, SHARD), 0) + i * ROWS == lax.broadcasted_iota(
                jnp.int32, (ROWS, SHARD), 1
            )
            scale = jnp.sum(jnp.where(here, scales[...], 0.0), axis=1, keepdims=True)
            momentum = of(0) * scale
            blended = beta_one * momentum + (1.0 - beta_one) * gradient
            root = lax.rsqrt(jnp.mean(blended * blended, axis=-1, keepdims=True) + epsilon)
            advanced = beta_two * momentum + (1.0 - beta_two) * gradient
            largest = jnp.max(jnp.abs(advanced), axis=-1, keepdims=True) + epsilon
            ww[rows_of(SHARD + i * ROWS, ROWS), :] = jnp.tanh(blended * root).astype(bf16)
            ww[rows_of(i * ROWS, ROWS), :] = (advanced * (1.0 / largest)).astype(bf16)
            new_scales[...] += jnp.sum(jnp.where(here, largest, 0.0), axis=0, keepdims=True)
            return carry

        lax.fori_loop(0, SHARD // ROWS, part, 0)
        for k in range(2):
            step_out(k).start()

    product_a(0)
    send(0)
    product_b(3)
    product_b(4)
    to_sibling(0).start()
    forward(0)
    ag[4].wait_recv()
    ag[11].start()
    ag[5].wait_recv()
    ag[12].start()
    product_a(1)
    send(1)
    add_sibling(0)
    far(0).start()
    far(1).start()
    product_a(2)
    send(2)
    product_b(0)
    forward(1)
    product_b(1)
    product_b(2)
    for k in range(1, 4):
        to_sibling(k).start()
    ag[11].wait_recv()
    ag[12].wait_recv()
    product_a(3)
    send(3)
    add_sibling(1)
    near(0, 1).start()
    add_sibling(2)
    near(1, 0).start()
    forward(2)
    add_far(0)
    near(0, 0).start()
    add_far(1)
    near(1, 1).start()
    product_a(4)
    send(4)
    add_sibling(3)

    for i in range(13):
        ag[i].wait_send()
    for d in (1, 2, 3):
        meta_copy(0, d).wait_send()
        meta_copy(1, d).wait_send()
        for j in range(4):
            p2a(j, d).wait_send()
            p2b(j, d).wait_send()
    step_load(0).start()

    pick(0)
    forward(3)
    pick(1)
    forward(4)
    pick(2)
    for i in range(2):
        for h in range(2):
            near(i, h).wait_recv()
    step_load(1).start()
    step_load(2).start()
    pick(3)
    step()
    pick(4)

    for k in range(4):
        to_sibling(k).wait_send()
    for i in range(2):
        far(i).wait_send()
        for h in range(2):
            near(i, h).wait_send()
    for j in range(NCH):
        for d in (1, 2, 3):
            r1a(j, d).wait_send()
            r1b(j, d).wait_send()
            r2a(j, d).wait_send()
            r2b(j, d).wait_send()
    for k in range(2):
        step_out(k).wait()
    out_copy(3).wait()
    out_copy(4).wait()


def main_call(factor, og, ids, gates, scales, w, hid, codes):
    any_spec = pl.BlockSpec(memory_space=pl.ANY)
    vmem = pl.BlockSpec(memory_space=pltpu.VMEM)
    dma = pltpu.SemaphoreType.DMA
    s = jax.ShapeDtypeStruct
    return pl.pallas_call(
        functools.partial(main_kernel, factor),
        out_shape=(
            s((TOK, 2, FF), bf16),
            s((SHARD, D), bf16),
            s((SHARD, D), bf16),
            s((1, SHARD), f32),
            s((NCH, 4, 4, CAP, C), bf16),
            s((2, SHARD, D), bf16),
            s((4, SHARD, D), bf16),
            s((NCH, 4, 4, HALF, C), bf16),
            s((NCH, 4, 4, HALF, C), bf16),
        ),
        in_specs=[vmem] * 4 + [any_spec] * 3,
        out_specs=[any_spec] * 3 + [vmem] + [any_spec] * 5,
        scratch_shapes=[
            pltpu.VMEM((4, 4, CAP, HD), bf16),
            pltpu.VMEM((4, 4, CAP, HD), bf16),
            pltpu.VMEM((8, 8, TOK), f32),
            pltpu.VMEM((4, 4, CAP, D), bf16),
            pltpu.VMEM((FF, D), bf16),
            pltpu.VMEM((16 * CAP, FF), bf16),
            pltpu.VMEM((FF, D), bf16),
            pltpu.VMEM((NCH, 4, 4, CAP, C), bf16),
            pltpu.VMEM((SHARD, D), bf16),
            pltpu.VMEM((SHARD, D), bf16),
            pltpu.VMEM((2 * TOK, 16 * CAP), bf16),
            pltpu.VMEM((2, TOK, 2, C), bf16),
            dma((13,)), dma((13,)), dma((9,)),
            dma((12,)), dma((12,)), dma((6,)), dma((6,)), dma((24,)), dma((24,)),
            dma((NCH, 6)), dma((NCH, 6)), dma((NCH, 6)), dma((NCH, 6)), dma((NCH, 4)),
            dma((4,)), dma((4,)), dma((6,)), dma((6,)), dma((2 * NCH + 5,)), dma((8,)),
        ],
        compiler_params=pltpu.CompilerParams(
            collective_id=0, has_side_effects=True, vmem_limit_bytes=63 * 2**20
        ),
        cost_estimate=pl.CostEstimate(flops=32 * 10**9, bytes_accessed=60 * 10**6, transcendentals=0),
        name="expert_backward",
    )(og, ids, gates, scales, w, hid, codes)


def place_kernel(grad, direction, codes, scales, grad_out, direction_out, codes_out, scales_out):
    grad_out[...] = grad[...]
    direction_out[...] = direction[...]
    codes_out[...] = codes[...]
    scales_out[...] = scales[...]


def place_call(*arrays):
    blocks = [
        pl.BlockSpec((TOK // 8, 2, FF), lambda i: (i, 0, 0)),
        pl.BlockSpec((SHARD, D // 8), lambda i: (0, i)),
        pl.BlockSpec((SHARD, D // 8), lambda i: (0, i)),
        pl.BlockSpec((1, SHARD), lambda i: (0, 0)),
    ]
    return pl.pallas_call(
        place_kernel,
        grid=(8,),
        out_shape=tuple(jax.ShapeDtypeStruct(a.shape, a.dtype) for a in arrays),
        in_specs=blocks,
        out_specs=blocks,
        name="place_outputs",
    )(*arrays)


def local(out_grad, expert_ids, gates, hidden_slots, weights, mom_codes, mom_scales):
    experts = lax.axis_size("expert")
    groups = lax.axis_size("dp")
    tokens_all = out_grad.shape[0] * groups * experts
    ids = expert_ids.T
    factor = math.sqrt(experts / (2.0 * tokens_all))
    results = main_call(
        factor, out_grad, ids, gates.T, mom_scales, weights[0], hidden_slots.reshape(16 * CAP, FF), mom_codes[0]
    )[:4]
    hidden_grad, direction, new_codes, new_scales = place_call(*results)
    return (hidden_grad, direction[None], new_codes[None], new_scales)


def solution(mesh):
    in_specs = (
        P(("dp", "expert"), None),
        P(("dp", "expert"), None),
        P(("dp", "expert"), None),
        P("dp", "expert", None, None, None),
        P("expert", "dp", None),
        P("expert", "dp", None),
        P("expert", "dp"),
    )
    out_specs = (
        P(("dp", "expert"), None, None),
        P("expert", "dp", None),
        P("expert", "dp", None),
        P("expert", "dp"),
    )
    return jax.shard_map(local, mesh=mesh, in_specs=in_specs, out_specs=out_specs, check_vma=False)
```

time: 174 us -> 155 us (0.89)
  Pallas kernels: 172 us -> 154 us
    pallas_call x3 -> x2, Pallas kernels: 172 us -> 154 us  [the longest x1 146 us: main_call(): pl.pallas_call(functools.partial(main_kernel, factor), out_shape=(s((TOK,...]
where the time goes in v2:
time: 155 us
  Pallas kernels  154 us (99%)
    pallas_call x1, Pallas kernels, main_call(): pl.pallas_call(functools.partial(main_kernel, factor), out_shape=(s((TOK,...  146 us
    pallas_call x1, Pallas kernels, place_call(): pl.pallas_call(place_kernel, grid=(8,), out_shape=tuple((jax.ShapeDtypeSt...  7.91 us

profile of v2, /device:TPU:0, one launch (start us, length us, event | category | flops | bytes accessed | tf_op | source)
XLA Modules:
  0.0 154.5 jit_solution(13540779226325394254)
XLA Ops:
  0.6 145.8 %expert_backward.1 = (bf16[256,2,3200]{2,1,0:T(2,128)(2,1)}, bf16[400,2048]{1,0:T(8,128)(2,1)}, bf16[400,2048]{1,0:T(8,128)(2,1)}, f32[1,400]{1,0:T(1,128)}, bf1...) custom-call(bf16[256,2048]{1,0:T(8,128)(2,1)} %og.1, ...), custom_call_target="tpu_custom_call" | custom-call | flops 32000000000 | bytes 60000000 | tf_op jit(solution)/shard_map/expert_backward/pallas_call | solution.py:532
  146.5 7.9 %place_outputs.1 = (bf16[256,2,3200]{2,1,0:T(2,128)(2,1)}, bf16[400,2048]{1,0:T(8,128)(2,1)}, bf16[400,2048]{1,0:T(8,128)(2,1)}, f32[1,400]{1,0:T(1,128)}) custom-call(bf16[256,2,3200]{2,1,0:T(2,128)(2,1)} %get-tuple-element.12.grad, bf16[400,2048]{1,0:T(8,128)(2,1)} %get-tuple-element.13.direction, bf16[400,2048]{1,0:T(8,128)(2,1)} %get-tuple-element.14.codes, ...), custom_call_target="tpu_custom_call" | custom-call | tf_op jit(solution)/shard_map/place_outputs/pallas_call | solution.py:587

commit v3 on v2

--- a/solution.py
+++ b/solution.py
@@ -53,7 +53,7 @@
     og, ids, gates, scales, w, hid, codes,
     hidden_grad, direction, new_codes, new_scales,
     ret, pieces, sr, m2a, m2b,
-    sa, sb, meta, rr, ww, hv, pb, oo, sums, tt, pk, ost,
+    sa, sb, meta, rr, ww, hv, pb, oo, sums, tt, pk, ost, last,
     ag_s, ag_r, loc, p1_s, p1_r, mt_s, mt_r, p2_s, p2_r, r1_s, r1_r, r2_s, r2_r, rl, sib_s, sib_r, x_s, x_r, tail_s, own_s,
 ):
     dp = lax.axis_index("dp")
@@ -243,19 +243,20 @@
     ag[3].wait_recv()
     ag[10].start()
 
-    for j in (0, 1, 3, 2):
-        for d in (1, 3, 2):
-            p2a(j, d).wait_recv()
-            p2b(j, d).wait_recv()
-        p2a_own(j).wait()
-        p2b_own(j).wait()
-    for i in range(6):
-        oy[i].wait_send()
-        oz[i].wait_send()
     w_own.wait()
     for i in range(6, 11):
         ag[i].wait_recv()
     h_load.wait()
+
+    def rows_here(d):
+        for k in (1, 3, 2):
+            p2a((4 - d) % 4, k).wait_recv()
+        p2a_own((4 - d) % 4).wait()
+        for j in (0, 1, 3, 2):
+            if d:
+                p2b(j, 4 - d).wait_recv()
+            else:
+                p2b_own(j).wait()
 
     first = ((x + 2) % 4 + 2) % 5
 
@@ -267,6 +268,13 @@
         rows = rr[...].reshape(16 * CAP, D)
         res = lax.dot_general(rows, wj, (((1,), (1,)), ((), ())), preferred_element_type=f32)
         oo[i] = res.astype(bf16).reshape(4, 4, CAP, C)
+
+    def product_first(d):
+        sy = (y + d) % 4
+        wj = ww[rows_of(chunk(0) * C, C), :]
+        rows = rr[sy].reshape(4 * CAP, D)
+        res = lax.dot_general(rows, wj, (((1,), (1,)), ((), ())), preferred_element_type=f32)
+        oo[0, sy] = res.astype(bf16).reshape(4, CAP, C)
 
     def product_b(i):
         at = chunk(i) * C
@@ -293,21 +301,24 @@
     def r1b_own(j):
         return pltpu.make_async_copy(oo.at[j, :, z, B, :], m2b.at[j, z], rl.at[j, 1])
 
+    def back(j):
+        return last if j == NCH - 1 else ret.at[chunk(j)]
+
     def r2a(j, d):
         return remote(
-            m2a.at[j, :, (z + d) % 4], ret.at[chunk(j), :, z, A, :], r2_s.at[j, d - 1], r2_r.at[j, d - 1], dev_z(d)
+            m2a.at[j, :, (z + d) % 4], back(j).at[:, z, A, :], r2_s.at[j, d - 1], r2_r.at[j, d - 1], dev_z(d)
         )
 
     def r2b(j, d):
         return remote(
-            m2b.at[j, :, (y + d) % 4], ret.at[chunk(j), y, :, B, :], r2_s.at[j, 2 + d], r2_r.at[j, 2 + d], dev_y(d)
+            m2b.at[j, :, (y + d) % 4], back(j).at[y, :, B, :], r2_s.at[j, 2 + d], r2_r.at[j, 2 + d], dev_y(d)
         )
 
     def r2a_own(j):
-        return pltpu.make_async_copy(m2a.at[j, :, z], ret.at[chunk(j), :, z, A, :], rl.at[j, 2])
+        return pltpu.make_async_copy(m2a.at[j, :, z], back(j).at[:, z, A, :], rl.at[j, 2])
 
     def r2b_own(j):
-        return pltpu.make_async_copy(m2b.at[j, :, y], ret.at[chunk(j), y, :, B, :], rl.at[j, 3])
+        return pltpu.make_async_copy(m2b.at[j, :, y], back(j).at[y, :, B, :], rl.at[j, 3])
 
     def send(j):
         for d in (1, 3, 2):
@@ -395,11 +406,12 @@
         for d in (1, 3, 2):
             r2a(i, d).wait_recv()
             r2b(i, d).wait_recv()
-        stage_load(i).start()
-        stage_load(i).wait()
+        if i < NCH - 1:
+            stage_load(i).start()
+            stage_load(i).wait()
         if i >= 2:
             out_copy(i - 2).wait()
-        rows = stage(i)[...].reshape(16 * CAP, C)
+        rows = (last if i == NCH - 1 else stage(i))[...].reshape(16 * CAP, C)
         got = jnp.dot(pk[...], rows, preferred_element_type=f32).astype(bf16)
         ost[i % 2, :, 0, :] = got[0:TOK]
         ost[i % 2, :, 1, :] = got[TOK:]
@@ -442,9 +454,22 @@
         for k in range(2):
             step_out(k).start()
 
-    product_a(0)
-    send(0)
+    rows_here(0)
+    product_first(0)
+    r1a_own(0).start()
+    for d in (1, 3, 2):
+        rows_here(d)
+        product_first(d)
+        r1a(0, d).start()
+    for d in (1, 3, 2):
+        r1b(0, d).start()
+    r1b_own(0).start()
+    for i in range(6):
+        oy[i].wait_send()
+        oz[i].wait_send()
     product_b(3)
+    product_a(1)
+    send(1)
     product_b(4)
     to_sibling(0).start()
     forward(0)
@@ -452,34 +477,32 @@
     ag[11].start()
     ag[5].wait_recv()
     ag[12].start()
-    product_a(1)
-    send(1)
+    product_b(0)
     add_sibling(0)
     far(0).start()
     far(1).start()
-    product_a(2)
-    send(2)
-    product_b(0)
-    forward(1)
     product_b(1)
     product_b(2)
     for k in range(1, 4):
         to_sibling(k).start()
+    product_a(2)
+    send(2)
+    forward(1)
+    add_sibling(1)
+    near(0, 1).start()
+    add_sibling(2)
+    near(1, 0).start()
     ag[11].wait_recv()
     ag[12].wait_recv()
     product_a(3)
     send(3)
-    add_sibling(1)
-    near(0, 1).start()
-    add_sibling(2)
-    near(1, 0).start()
-    forward(2)
     add_far(0)
     near(0, 0).start()
     add_far(1)
     near(1, 1).start()
     product_a(4)
     send(4)
+    forward(2)
     add_sibling(3)
 
     for i in range(13):
@@ -557,6 +580,7 @@
             pltpu.VMEM((SHARD, D), bf16),
             pltpu.VMEM((2 * TOK, 16 * CAP), bf16),
             pltpu.VMEM((2, TOK, 2, C), bf16),
+            pltpu.VMEM((4, 4, CAP, C), bf16),
             dma((13,)), dma((13,)), dma((9,)),
             dma((12,)), dma((12,)), dma((6,)), dma((6,)), dma((24,)), dma((24,)),
             dma((NCH, 6)), dma((NCH, 6)), dma((NCH, 6)), dma((NCH, 6)), dma((NCH, 4)),
@@ -570,26 +594,43 @@
     )(og, ids, gates, scales, w, hid, codes)
 
 
-def place_kernel(grad, direction, codes, scales, grad_out, direction_out, codes_out, scales_out):
-    grad_out[...] = grad[...]
-    direction_out[...] = direction[...]
-    codes_out[...] = codes[...]
-    scales_out[...] = scales[...]
+PARTS = 8
+
+
+def place_kernel(*refs):
+    sources, outputs, buffers, sems = refs[0:4], refs[4:8], refs[8:12], refs[12]
+
+    def views(ref, k):
+        if k:
+            return [ref]
+        return [ref.at[pl.ds(i * (TOK // PARTS), TOK // PARTS)] for i in range(PARTS)]
+
+    pairs = []
+    for k in range(4):
+        for src, buf, dst in zip(views(sources[k], k), views(buffers[k], k), views(outputs[k], k)):
+            i = len(pairs)
+            pairs.append(
+                (pltpu.make_async_copy(src, buf, sems.at[0, i]), pltpu.make_async_copy(buf, dst, sems.at[1, i]))
+            )
+    for load, _ in pairs:
+        load.start()
+    for load, store in pairs:
+        load.wait()
+        store.start()
+    for _, store in pairs:
+        store.wait()
 
 
 def place_call(*arrays):
-    blocks = [
-        pl.BlockSpec((TOK // 8, 2, FF), lambda i: (i, 0, 0)),
-        pl.BlockSpec((SHARD, D // 8), lambda i: (0, i)),
-        pl.BlockSpec((SHARD, D // 8), lambda i: (0, i)),
-        pl.BlockSpec((1, SHARD), lambda i: (0, 0)),
-    ]
+    hbm = pl.BlockSpec(memory_space=pltpu.HBM)
     return pl.pallas_call(
         place_kernel,
-        grid=(8,),
         out_shape=tuple(jax.ShapeDtypeStruct(a.shape, a.dtype) for a in arrays),
-        in_specs=blocks,
-        out_specs=blocks,
+        in_specs=[hbm] * 4,
+        out_specs=[hbm] * 4,
+        scratch_shapes=[pltpu.VMEM(a.shape, a.dtype) for a in arrays]
+        + [pltpu.SemaphoreType.DMA((2, PARTS + 3))],
+        compiler_params=pltpu.CompilerParams(vmem_limit_bytes=63 * 2**20),
         name="place_outputs",
     )(*arrays)
 

time: 155 us -> 146 us (0.942)
  Pallas kernels: 154 us -> 144 us
    pallas_call x1, Pallas kernels: 146 us -> 139 us  [main_call(): pl.pallas_call(functools.partial(main_kernel, factor), out_shape=(s((TOK,...]
    pallas_call x1, Pallas kernels: 7.91 us -> 5.48 us  [place_call(): pl.pallas_call(place_kernel, out_shape=tuple((jax.ShapeDtypeStruct(a.shap...]
where the time goes in v3:
time: 146 us; the launch traced here: 145 us
  Pallas kernels  144 us (99%)
    pallas_call x1, Pallas kernels, main_call(): pl.pallas_call(functools.partial(main_kernel, factor), out_shape=(s((TOK,...  139 us
    pallas_call x1, Pallas kernels, place_call(): pl.pallas_call(place_kernel, out_shape=tuple((jax.ShapeDtypeStruct(a.shap...  5.48 us

profile of v3, /device:TPU:0, one launch (start us, length us, event | category | flops | bytes accessed | tf_op | source)
XLA Modules:
  0.0 145.3 jit_solution(12313444997929240772)
XLA Ops:
  0.6 139.0 %expert_backward.1 = (bf16[256,2,3200]{2,1,0:T(2,128)(2,1)}, bf16[400,2048]{1,0:T(8,128)(2,1)}, bf16[400,2048]{1,0:T(8,128)(2,1)}, f32[1,400]{1,0:T(1,128)}, bf1...) custom-call(bf16[256,2048]{1,0:T(8,128)(2,1)} %og.1, ...), custom_call_target="tpu_custom_call" | custom-call | flops 32000000000 | bytes 60000000 | tf_op jit(solution)/shard_map/expert_backward/pallas_call | solution.py:555
  139.6 5.5 %place_outputs.1 = (bf16[256,2,3200]{2,1,0:T(2,128)(2,1)}, bf16[400,2048]{1,0:T(8,128)(2,1)}, bf16[400,2048]{1,0:T(8,128)(2,1)}, f32[1,400]{1,0:T(1,128)}) custom-call(bf16[256,2,3200]{2,1,0:T(2,128)(2,1)} %get-tuple-element.12.refs_0_, bf16[400,2048]{1,0:T(8,128)(2,1)} %get-tuple-element.13.refs_1_, bf16[400,2048]{1,0:T(8,128)(2,1)} %get-tuple-element.14.refs_2_, ...), custom_call_target="tpu_custom_call" | custom-call | tf_op jit(solution)/shard_map/place_outputs/pallas_call | solution.py:626

commit v4 on v3

--- a/solution.py
+++ b/solution.py
@@ -49,9 +49,8 @@
 
 
 def main_kernel(
-    factor,
-    og, ids, gates, scales, w, hid, codes,
-    hidden_grad, direction, new_codes, new_scales,
+    og, ids, gates, w, hid,
+    hidden_grad,
     ret, pieces, sr, m2a, m2b,
     sa, sb, meta, rr, ww, hv, pb, oo, sums, tt, pk, ost, last,
     ag_s, ag_r, loc, p1_s, p1_r, mt_s, mt_r, p2_s, p2_r, r1_s, r1_r, r2_s, r2_r, rl, sib_s, sib_r, x_s, x_r, tail_s, own_s,
@@ -417,42 +416,7 @@
         ost[i % 2, :, 1, :] = got[TOK:]
         out_copy(i).start()
 
-    def step_load(k):
-        src = (codes, pieces.at[0], pieces.at[1])[k]
-        return pltpu.make_async_copy(src, ww.at[pl.ds(k * SHARD, SHARD)], tail_s.at[2 * NCH + k])
-
-    def step_out(k):
-        dst = (new_codes, direction)[k]
-        return pltpu.make_async_copy(ww.at[pl.ds(k * SHARD, SHARD)], dst, tail_s.at[2 * NCH + 3 + k])
-
-    def step():
-        for k in range(3):
-            step_load(k).wait()
-        new_scales[...] = jnp.zeros_like(new_scales)
-
-        def part(i, carry):
-            def of(k):
-                return ww[rows_of(k * SHARD + i * ROWS, ROWS), :].astype(f32)
-
-            mine = pb[shard_rows(x, c, i * ROWS, ROWS), :].astype(f32)
-            gradient = factor * (mine + of(1) + of(2))
-            here = lax.broadcasted_iota(jnp.int32, (ROWS, SHARD), 0) + i * ROWS == lax.broadcasted_iota(
-                jnp.int32, (ROWS, SHARD), 1
-            )
-            scale = jnp.sum(jnp.where(here, scales[...], 0.0), axis=1, keepdims=True)
-            momentum = of(0) * scale
-            blended = beta_one * momentum + (1.0 - beta_one) * gradient
-            root = lax.rsqrt(jnp.mean(blended * blended, axis=-1, keepdims=True) + epsilon)
-            advanced = beta_two * momentum + (1.0 - beta_two) * gradient
-            largest = jnp.max(jnp.abs(advanced), axis=-1, keepdims=True) + epsilon
-            ww[rows_of(SHARD + i * ROWS, ROWS), :] = jnp.tanh(blended * root).astype(bf16)
-            ww[rows_of(i * ROWS, ROWS), :] = (advanced * (1.0 / largest)).astype(bf16)
-            new_scales[...] += jnp.sum(jnp.where(here, largest, 0.0), axis=0, keepdims=True)
-            return carry
-
-        lax.fori_loop(0, SHARD // ROWS, part, 0)
-        for k in range(2):
-            step_out(k).start()
+    own_piece = pltpu.make_async_copy(pb.at[shard_rows(x, c, 0, SHARD)], pieces.at[2], tail_s.at[2 * NCH])
 
     rows_here(0)
     product_first(0)
@@ -481,29 +445,30 @@
     add_sibling(0)
     far(0).start()
     far(1).start()
+    product_a(2)
+    send(2)
+    forward(1)
     product_b(1)
     product_b(2)
     for k in range(1, 4):
         to_sibling(k).start()
-    product_a(2)
-    send(2)
-    forward(1)
+    ag[11].wait_recv()
+    ag[12].wait_recv()
+    product_a(3)
+    send(3)
     add_sibling(1)
     near(0, 1).start()
     add_sibling(2)
     near(1, 0).start()
-    ag[11].wait_recv()
-    ag[12].wait_recv()
-    product_a(3)
-    send(3)
+    forward(2)
     add_far(0)
     near(0, 0).start()
     add_far(1)
     near(1, 1).start()
     product_a(4)
     send(4)
-    forward(2)
     add_sibling(3)
+    own_piece.start()
 
     for i in range(13):
         ag[i].wait_send()
@@ -513,20 +478,12 @@
         for j in range(4):
             p2a(j, d).wait_send()
             p2b(j, d).wait_send()
-    step_load(0).start()
-
     pick(0)
     forward(3)
     pick(1)
     forward(4)
     pick(2)
-    for i in range(2):
-        for h in range(2):
-            near(i, h).wait_recv()
-    step_load(1).start()
-    step_load(2).start()
     pick(3)
-    step()
     pick(4)
 
     for k in range(4):
@@ -534,39 +491,35 @@
     for i in range(2):
         far(i).wait_send()
         for h in range(2):
-            near(i, h).wait_send()
+            near(i, h).wait()
     for j in range(NCH):
         for d in (1, 2, 3):
             r1a(j, d).wait_send()
             r1b(j, d).wait_send()
             r2a(j, d).wait_send()
             r2b(j, d).wait_send()
-    for k in range(2):
-        step_out(k).wait()
+    own_piece.wait()
     out_copy(3).wait()
     out_copy(4).wait()
 
 
-def main_call(factor, og, ids, gates, scales, w, hid, codes):
+def main_call(og, ids, gates, w, hid):
     any_spec = pl.BlockSpec(memory_space=pl.ANY)
     vmem = pl.BlockSpec(memory_space=pltpu.VMEM)
     dma = pltpu.SemaphoreType.DMA
     s = jax.ShapeDtypeStruct
     return pl.pallas_call(
-        functools.partial(main_kernel, factor),
+        main_kernel,
         out_shape=(
             s((TOK, 2, FF), bf16),
-            s((SHARD, D), bf16),
-            s((SHARD, D), bf16),
-            s((1, SHARD), f32),
             s((NCH, 4, 4, CAP, C), bf16),
-            s((2, SHARD, D), bf16),
+            s((3, SHARD, D), bf16),
             s((4, SHARD, D), bf16),
             s((NCH, 4, 4, HALF, C), bf16),
             s((NCH, 4, 4, HALF, C), bf16),
         ),
-        in_specs=[vmem] * 4 + [any_spec] * 3,
-        out_specs=[any_spec] * 3 + [vmem] + [any_spec] * 5,
+        in_specs=[vmem] * 3 + [any_spec] * 2,
+        out_specs=[any_spec] * 6,
         scratch_shapes=[
             pltpu.VMEM((4, 4, CAP, HD), bf16),
             pltpu.VMEM((4, 4, CAP, HD), bf16),
@@ -591,48 +544,99 @@
         ),
         cost_estimate=pl.CostEstimate(flops=32 * 10**9, bytes_accessed=60 * 10**6, transcendentals=0),
         name="expert_backward",
-    )(og, ids, gates, scales, w, hid, codes)
+    )(og, ids, gates, w, hid)
 
 
 PARTS = 8
-
-
-def place_kernel(*refs):
-    sources, outputs, buffers, sems = refs[0:4], refs[4:8], refs[8:12], refs[12]
-
-    def views(ref, k):
-        if k:
-            return [ref]
-        return [ref.at[pl.ds(i * (TOK // PARTS), TOK // PARTS)] for i in range(PARTS)]
-
-    pairs = []
-    for k in range(4):
-        for src, buf, dst in zip(views(sources[k], k), views(buffers[k], k), views(outputs[k], k)):
-            i = len(pairs)
-            pairs.append(
-                (pltpu.make_async_copy(src, buf, sems.at[0, i]), pltpu.make_async_copy(buf, dst, sems.at[1, i]))
-            )
-    for load, _ in pairs:
+STEPS = SHARD // ROWS
+
+
+def finish_kernel(
+    factor, grad, pieces, codes, scales, grad_out, direction, new_codes, new_scales, gbuf, pbuf, cbuf, dbuf, gsem, ssem
+):
+    def grad_rows(ref, i):
+        return ref.at[pl.ds(i * (TOK // PARTS), TOK // PARTS)]
+
+    grad_loads = [
+        pltpu.make_async_copy(grad_rows(grad, i), grad_rows(gbuf, i), gsem.at[0, i]) for i in range(PARTS)
+    ]
+    grad_stores = [
+        pltpu.make_async_copy(grad_rows(gbuf, i), grad_rows(grad_out, i), gsem.at[1, i]) for i in range(PARTS)
+    ]
+    at = [pl.ds(i * ROWS, ROWS) for i in range(STEPS)]
+    loads = [
+        (
+            pltpu.make_async_copy(pieces.at[:, r], pbuf.at[:, r], ssem.at[0, i]),
+            pltpu.make_async_copy(codes.at[r], cbuf.at[r], ssem.at[1, i]),
+        )
+        for i, r in enumerate(at)
+    ]
+    stores = [
+        (
+            pltpu.make_async_copy(dbuf.at[r], direction.at[r], ssem.at[2, i]),
+            pltpu.make_async_copy(cbuf.at[r], new_codes.at[r], ssem.at[3, i]),
+        )
+        for i, r in enumerate(at)
+    ]
+    for pair in loads[:2]:
+        for load in pair:
+            load.start()
+    for load in grad_loads:
         load.start()
-    for load, store in pairs:
-        load.wait()
-        store.start()
-    for _, store in pairs:
+    for pair in loads[2:]:
+        for load in pair:
+            load.start()
+    scale_row = scales[...]
+    largest_row = jnp.zeros((1, SHARD), f32)
+    for i, r in enumerate(at):
+        for load in loads[i]:
+            load.wait()
+        gradient = factor * (pbuf[0, r, :].astype(f32) + pbuf[1, r, :].astype(f32) + pbuf[2, r, :].astype(f32))
+        here = lax.broadcasted_iota(jnp.int32, (ROWS, SHARD), 0) + i * ROWS == lax.broadcasted_iota(
+            jnp.int32, (ROWS, SHARD), 1
+        )
+        scale = jnp.sum(jnp.where(here, scale_row, 0.0), axis=1, keepdims=True)
+        momentum = cbuf[r, :].astype(f32) * scale
+        blended = beta_one * momentum + (1.0 - beta_one) * gradient
+        root = lax.rsqrt(jnp.mean(blended * blended, axis=-1, keepdims=True) + epsilon)
+        advanced = beta_two * momentum + (1.0 - beta_two) * gradient
+        largest = jnp.max(jnp.abs(advanced), axis=-1, keepdims=True) + epsilon
+        dbuf[r, :] = jnp.tanh(blended * root).astype(bf16)
+        cbuf[r, :] = (advanced * (1.0 / largest)).astype(bf16)
+        largest_row += jnp.sum(jnp.where(here, largest, 0.0), axis=0, keepdims=True)
+        for store in stores[i]:
+            store.start()
+        for k in range(2 * i, min(2 * i + 2, PARTS)):
+            grad_loads[k].wait()
+            grad_stores[k].start()
+    new_scales[...] = largest_row
+    for pair in stores:
+        for store in pair:
+            store.wait()
+    for store in grad_stores:
         store.wait()
 
 
-def place_call(*arrays):
+def finish_call(factor, grad, pieces, codes, scales):
     hbm = pl.BlockSpec(memory_space=pltpu.HBM)
+    vmem = pl.BlockSpec(memory_space=pltpu.VMEM)
+    s = jax.ShapeDtypeStruct
     return pl.pallas_call(
-        place_kernel,
-        out_shape=tuple(jax.ShapeDtypeStruct(a.shape, a.dtype) for a in arrays),
-        in_specs=[hbm] * 4,
-        out_specs=[hbm] * 4,
-        scratch_shapes=[pltpu.VMEM(a.shape, a.dtype) for a in arrays]
-        + [pltpu.SemaphoreType.DMA((2, PARTS + 3))],
+        functools.partial(finish_kernel, factor),
+        out_shape=(s(grad.shape, bf16), s((SHARD, D), bf16), s((SHARD, D), bf16), s((1, SHARD), f32)),
+        in_specs=[hbm, hbm, hbm, vmem],
+        out_specs=[hbm, hbm, hbm, vmem],
+        scratch_shapes=[
+            pltpu.VMEM(grad.shape, bf16),
+            pltpu.VMEM((3, SHARD, D), bf16),
+            pltpu.VMEM((SHARD, D), bf16),
+            pltpu.VMEM((SHARD, D), bf16),
+            pltpu.SemaphoreType.DMA((2, PARTS)),
+            pltpu.SemaphoreType.DMA((4, STEPS)),
+        ],
         compiler_params=pltpu.CompilerParams(vmem_limit_bytes=63 * 2**20),
-        name="place_outputs",
-    )(*arrays)
+        name="step_and_place",
+    )(grad, pieces, codes, scales)
 
 
 def local(out_grad, expert_ids, gates, hidden_slots, weights, mom_codes, mom_scales):
@@ -641,10 +645,12 @@
     tokens_all = out_grad.shape[0] * groups * experts
     ids = expert_ids.T
     factor = math.sqrt(experts / (2.0 * tokens_all))
-    results = main_call(
-        factor, out_grad, ids, gates.T, mom_scales, weights[0], hidden_slots.reshape(16 * CAP, FF), mom_codes[0]
-    )[:4]
-    hidden_grad, direction, new_codes, new_scales = place_call(*results)
+    hidden_grad, _, pieces = main_call(
+        out_grad, ids, gates.T, weights[0], hidden_slots.reshape(16 * CAP, FF)
+    )[:3]
+    hidden_grad, direction, new_codes, new_scales = finish_call(
+        factor, hidden_grad, pieces, mom_codes[0], mom_scales
+    )
     return (hidden_grad, direction[None], new_codes[None], new_scales)
 
 

time: 146 us -> 141 us (0.966)
  Pallas kernels: 144 us -> 139 us
    pallas_call x2, Pallas kernels: 144 us -> 139 us  [the longest x1 131 us: main_call(): pl.pallas_call(main_kernel, out_shape=(s((TOK, 2, FF), bf16), s((NCH, 4,...]
where the time goes in v4:
time: 141 us; the launch traced here: 140 us
  Pallas kernels  139 us (99%)
    pallas_call x1, Pallas kernels, main_call(): pl.pallas_call(main_kernel, out_shape=(s((TOK, 2, FF), bf16), s((NCH, 4,...  131 us
    pallas_call x1, Pallas kernels, finish_call(): pl.pallas_call(functools.partial(finish_kernel, factor), out_shape=(s(gra...  8.31 us

profile of v4, /device:TPU:0, one launch (start us, length us, event | category | flops | bytes accessed | tf_op | source)
XLA Modules:
  0.0 140.2 jit_solution(16607461258017860352)
XLA Ops:
  0.6 131.0 %expert_backward.1 = (bf16[256,2,3200]{2,1,0:T(2,128)(2,1)}, bf16[5,4,4,64,640]{4,3,2,1,0:T(8,128)(2,1)}, bf16[3,400,2048]{2,1,0:T(8,128)(2,1)}, bf16[4,400,2048...) custom-call(bf16[256,2048]{1,0:T(8,128)(2,1)} %og.1, s32[2,256]{1,0:T(2,128)} %bitcast.12, ...), custom_call_target="tpu_custom_call" | custom-call | flops 32000000000 | bytes 60000000 | tf_op jit(solution)/shard_map/expert_backward/pallas_call | solution.py:511
  131.7 8.3 %step_and_place.1 = (bf16[256,2,3200]{2,1,0:T(2,128)(2,1)}, bf16[400,2048]{1,0:T(8,128)(2,1)}, bf16[400,2048]{1,0:T(8,128)(2,1)}, f32[1,400]{1,0:T(1,128)}) custom-call(bf16[256,2,3200]{2,1,0:T(2,128)(2,1)} %get-tuple-element.10.grad, bf16[3,400,2048]{2,1,0:T(8,128)(2,1)} %get-tuple-element.11.pieces, bf16[400,2048]{1,0:T(8,128)(2,1)} %bitcast.7, ...), custom_call_target="tpu_custom_call" | custom-call | tf_op jit(solution)/shard_map/step_and_place/pallas_call | solution.py:624

commit v5 on v4

--- a/solution.py
+++ b/solution.py
@@ -478,8 +478,8 @@
         for j in range(4):
             p2a(j, d).wait_send()
             p2b(j, d).wait_send()
+    forward(3)
     pick(0)
-    forward(3)
     pick(1)
     forward(4)
     pick(2)
@@ -578,28 +578,25 @@
         )
         for i, r in enumerate(at)
     ]
-    for pair in loads[:2]:
+    for pair in loads:
         for load in pair:
             load.start()
     for load in grad_loads:
         load.start()
-    for pair in loads[2:]:
-        for load in pair:
-            load.start()
     scale_row = scales[...]
     largest_row = jnp.zeros((1, SHARD), f32)
     for i, r in enumerate(at):
         for load in loads[i]:
             load.wait()
-        gradient = factor * (pbuf[0, r, :].astype(f32) + pbuf[1, r, :].astype(f32) + pbuf[2, r, :].astype(f32))
+        summed = pbuf[0, r, :].astype(f32) + pbuf[1, r, :].astype(f32) + pbuf[2, r, :].astype(f32)
         here = lax.broadcasted_iota(jnp.int32, (ROWS, SHARD), 0) + i * ROWS == lax.broadcasted_iota(
             jnp.int32, (ROWS, SHARD), 1
         )
         scale = jnp.sum(jnp.where(here, scale_row, 0.0), axis=1, keepdims=True)
-        momentum = cbuf[r, :].astype(f32) * scale
-        blended = beta_one * momentum + (1.0 - beta_one) * gradient
+        coded = cbuf[r, :].astype(f32)
+        blended = coded * (beta_one * scale) + ((1.0 - beta_one) * factor) * summed
         root = lax.rsqrt(jnp.mean(blended * blended, axis=-1, keepdims=True) + epsilon)
-        advanced = beta_two * momentum + (1.0 - beta_two) * gradient
+        advanced = coded * (beta_two * scale) + ((1.0 - beta_two) * factor) * summed
         largest = jnp.max(jnp.abs(advanced), axis=-1, keepdims=True) + epsilon
         dbuf[r, :] = jnp.tanh(blended * root).astype(bf16)
         cbuf[r, :] = (advanced * (1.0 / largest)).astype(bf16)

time: 141 us -> 141 us (level)
  no operation moved by 1% of the time
where the time goes in v5:
time: 141 us; the launch traced here: 140 us
  Pallas kernels  139 us (99%)
    pallas_call x1, Pallas kernels, main_call(): pl.pallas_call(main_kernel, out_shape=(s((TOK, 2, FF), bf16), s((NCH, 4,...  131 us
    pallas_call x1, Pallas kernels, finish_call(): pl.pallas_call(functools.partial(finish_kernel, factor), out_shape=(s(gra...  8.22 us

profile of v5, /device:TPU:0, one launch (start us, length us, event | category | flops | bytes accessed | tf_op | source)
XLA Modules:
  0.0 140.1 jit_solution(13264422428785563130)
XLA Ops:
  0.6 131.0 %expert_backward.1 = (bf16[256,2,3200]{2,1,0:T(2,128)(2,1)}, bf16[5,4,4,64,640]{4,3,2,1,0:T(8,128)(2,1)}, bf16[3,400,2048]{2,1,0:T(8,128)(2,1)}, bf16[4,400,2048...) custom-call(bf16[256,2048]{1,0:T(8,128)(2,1)} %og.1, s32[2,256]{1,0:T(2,128)} %bitcast.12, ...), custom_call_target="tpu_custom_call" | custom-call | flops 32000000000 | bytes 60000000 | tf_op jit(solution)/shard_map/expert_backward/pallas_call | solution.py:511
  131.7 8.2 %step_and_place.1 = (bf16[256,2,3200]{2,1,0:T(2,128)(2,1)}, bf16[400,2048]{1,0:T(8,128)(2,1)}, bf16[400,2048]{1,0:T(8,128)(2,1)}, f32[1,400]{1,0:T(1,128)}) custom-call(bf16[256,2,3200]{2,1,0:T(2,128)(2,1)} %get-tuple-element.10.grad, bf16[3,400,2048]{2,1,0:T(8,128)(2,1)} %get-tuple-element.11.pieces, bf16[400,2048]{1,0:T(8,128)(2,1)} %bitcast.7, ...), custom_call_target="tpu_custom_call" | custom-call | tf_op jit(solution)/shard_map/step_and_place/pallas_call | solution.py:621
